TPU v7x, 128 devices: a whole 4x4x4 slice. The times are simulated.
128 devices in a mesh: hst: 16 (over y, x), chip: 8 (over z, core).
Axes of the slice: x: 4, y: 4, z: 4, core: 2. Of those that a mesh axis runs over, the one named last changes fastest.
Arguments:
- tile_data: bfloat16 [4096, 512, 512], P(('hst', 'chip')), may hold values from -0.09375 to 0.09375
- tile_col: int32 [4096], P(('hst', 'chip')), may hold values from 0 to 127, as said below
- live_count: int32 [128], P(('hst', 'chip')), may hold values from 16 to 32, as said below
- degree: int32 [65536], P(('hst', 'chip')), may hold values from 1 to 100
- start_basis: bfloat16 [65536, 128], P(('hst', 'chip')), may hold values from -6 to 6
Outputs:
- leading_basis: float32 [65536, 128], P(('hst', 'chip'))
- factor: float32 [128, 128], replicated
Inputs may be any that keep to these rules, and one draw needn't show every extreme that they name: `tile_col`: slot 0 of every row block names that block itself. `live_count`: some row block has all 32 slots live in every draw.
All inputs are finite; a program needn't handle non-finite values.
Results may differ from a plain program's by a relative error of at most 0.019.
Values may be sent and summed in bfloat16 or wider, within the bound.
A program may use at most 128 MiB of HBM per device.

v0:
```python
import jax
import jax.numpy as jnp
from jax import lax
from jax.sharding import PartitionSpec as P

BLK = 512
K = 128


def fetch_basis(scaled):
    return lax.all_gather(scaled, ("hst", "chip"), axis=0, tiled=True)


def apply_tiles(tile_data, tile_col, live_count, gathered, row_scale):
    block_total = gathered.shape[0] // BLK
    blocks = gathered.reshape(block_total, BLK, K)
    width_group = 4
    rounds = (live_count[0] + width_group - 1) // width_group

    def add_group(turn, running):
        first_slot = turn * width_group
        tile_part = lax.dynamic_slice_in_dim(tile_data, first_slot, width_group, 0)
        columns = lax.dynamic_slice_in_dim(tile_col, first_slot, width_group, 0)
        picked = blocks[columns]
        product = jnp.einsum("sij,sjk->sik", tile_part, picked, preferred_element_type=jnp.float32)
        living = (first_slot + jnp.arange(width_group, dtype=jnp.int32) < live_count[0]).astype(
            jnp.float32
        )
        return running + jnp.einsum("s,sik->ik", living, product)

    running = lax.fori_loop(0, rounds, add_group, jnp.zeros((BLK, K), jnp.float32))
    return running * row_scale[:, None]


def factor_inverse(gram_matrix):
    lower_factor = jnp.linalg.cholesky(gram_matrix)
    identity = jnp.eye(gram_matrix.shape[0], dtype=jnp.float32)
    inverse = lax.linalg.triangular_solve(lower_factor, identity, left_side=True, lower=True)
    return (lower_factor, inverse)


def local_gram(matrix, item_total):
    return jnp.dot(matrix.T, matrix, precision=lax.Precision.HIGHEST) / item_total


def local(tile_data, tile_col, live_count, degree, start_basis):
    item_total = BLK * lax.axis_size("hst") * lax.axis_size("chip")
    row_scale = 1.0 / jnp.sqrt(degree.astype(jnp.float32))
    start_scaled = (row_scale[:, None] * start_basis.astype(jnp.float32)).astype(jnp.bfloat16)
    first_image = apply_tiles(tile_data, tile_col, live_count, fetch_basis(start_scaled), row_scale)
    mid_scaled = (row_scale[:, None] * first_image).astype(jnp.bfloat16)
    first_gram = lax.psum(local_gram(first_image, item_total), ("hst", "chip"))
    lower_one, inverse_one = factor_inverse(first_gram)
    raw_second = apply_tiles(tile_data, tile_col, live_count, fetch_basis(mid_scaled), row_scale)
    second = jnp.dot(raw_second, inverse_one.T, precision=lax.Precision.HIGHEST)
    second_gram = lax.psum(local_gram(second, item_total), ("hst", "chip"))
    factor, inverse_two = factor_inverse(second_gram)
    leading_basis = jnp.dot(second, inverse_two.T, precision=lax.Precision.HIGHEST)
    return (leading_basis, factor)


def solution(mesh):
    placed = (
        P(("hst", "chip"), None, None),
        P(("hst", "chip")),
        P(("hst", "chip")),
        P(("hst", "chip")),
        P(("hst", "chip"), None),
    )
    return jax.shard_map(
        local,
        mesh=mesh,
        in_specs=placed,
        out_specs=(P(("hst", "chip"), None), P()),
        check_vma=False,
    )
```

profile of v0, /device:TPU:1, one launch (start us, length us, event | category | flops | bytes accessed | tf_op | source)
XLA Modules:
  0.0 659.0 jit_solution(7971596536017122263)
XLA Ops:
  10.3 85.4 %all-gather.3.cloned.1.call-done = bf16[65536,128]{1,0:T(8,128)(2,1)} async-done(((bf16[512,128]{1,0:T(8,128)(2,1)}), bf16[65536,128]{1,0:T(8,128)(2,1)}) %all-gather.3.cloned.1.call-update) | async-done | bytes 16777232 | tf_op jit(solution)/shard_map/all_gather | solution.py:11
  95.8 42.8 %while.20 = (s32[]{:T(128)}, f32[512,128]{1,0:T(8,128)S(1)}, s32[]{:T(128)}, s32[1]{0:T(128)}, bf16[32,512,512]{2,1,0:T(8,128)(2,1)}, /*index=5*/s32[32]{0:T(128...) while((s32[]{:T(128)}, f32[512,128]{1,0:T(8,128)S(1)}, ...), condition=%wide.region_1.2_spmd, body=%wide.region_0.1_spmd.sunk | while | flops 269026336 | bytes 5771499 | solution.py:31
  96.5 6.4 gather_fusion
  103.0 2.3 fusion.60
  107.2 6.4 gather_fusion
  113.7 2.3 fusion.60
  117.9 6.4 gather_fusion
  128.6 6.4 gather_fusion
  140.9 178.5 %all-reduce.3.cloned.1.call-done = f32[128,128]{0,1:T(8,128)} async-done(((f32[128,128]{0,1:T(8,128)}), f32[128,128]{0,1:T(8,128)}) %all-reduce.3.cloned.1.call-update) | async-done | bytes 65552 | tf_op jit(solution)/shard_map/psum | solution.py:52
  321.2 11.7 %cholesky.44 = f32[128,128]{1,0:T(8,128)S(1)} custom-call(f32[128,128]{1,0:T(8,128)S(1)} %fusion.35), custom_call_target="Cholesky" | custom-call | tf_op jit(solution)/shard_map/jit(cholesky)/cholesky | solution.py:36
  334.3 9.8 %custom-call.6 = f32[1,128,128]{1,2,0:T(8,128)S(1)} custom-call(f32[1,128,128]{2,1,0:T(8,128)S(1)} %fusion.31), custom_call_target="InvertDiagBlocksLowerTriangular" | custom-call | tf_op jit(solution)/shard_map/triangular_solve/custom-call.0 | solution.py:38
  344.4 57.4 %all-gather.5.cloned.1.call-done = bf16[65536,128]{1,0:T(8,128)(2,1)} async-done(((bf16[512,128]{1,0:T(8,128)(2,1)}), bf16[65536,128]{1,0:T(8,128)(2,1)}) %all-gather.5.cloned.1.call-update) | async-done | bytes 16777232 | tf_op jit(solution)/shard_map/all_gather | solution.py:11
  401.8 43.0 %while.21 = (s32[]{:T(128)}, f32[512,128]{1,0:T(8,128)S(1)}, s32[]{:T(128)}, s32[1]{0:T(128)}, bf16[32,512,512]{2,1,0:T(8,128)(2,1)}, /*index=5*/s32[32]{0:T(128...) while((s32[]{:T(128)}, f32[512,128]{1,0:T(8,128)S(1)}, ...), condition=%wide.region_3.4_spmd, body=%wide.region_2.3_spmd.sunk | while | flops 269026336 | bytes 5771499 | solution.py:31
  402.6 6.4 gather_fusion.1
  409.0 2.3 fusion.66
  413.2 6.4 gather_fusion.1
  419.7 2.3 fusion.66
  423.9 6.4 gather_fusion.1
  430.4 2.3 fusion.66
  434.6 6.4 gather_fusion.1
  441.1 2.3 fusion.66
  446.4 179.4 %all-reduce.5.cloned.1.call-done = f32[128,128]{0,1:T(8,128)} async-done(((f32[128,128]{0,1:T(8,128)}), f32[128,128]{0,1:T(8,128)}) %all-reduce.5.cloned.1.call-update) | async-done | bytes 65552 | tf_op jit(solution)/shard_map/psum | solution.py:56
  627.6 11.7 %cholesky.55 = f32[128,128]{1,0:T(8,128)S(1)} custom-call(f32[128,128]{1,0:T(8,128)S(1)} %fusion.33), custom_call_target="Cholesky" | custom-call | tf_op jit(solution)/shard_map/jit(cholesky)/cholesky | solution.py:36
  641.3 9.8 %custom-call.7 = f32[1,128,128]{1,2,0:T(8,128)S(1)} custom-call(f32[1,128,128]{2,1,0:T(8,128)S(1)} %get-tuple-element.110), custom_call_target="InvertDiagBlocksLowerTriangular" | custom-call | tf_op jit(solution)/shard_map/triangular_solve/custom-call.0 | solution.py:38
  (63 shorter events, 35.0 us)
Async XLA Ops:
  7.2 88.6 %all-gather.3.cloned.1.call-start = ((), (), s32[]{:S(2)}) async-start(), calls=%async_computation | async-start | bytes 16908288 | tf_op jit(solution)/shard_map/all_gather | solution.py:11
  9.6 309.8 %all-reduce.3.cloned.1.call-start = ((), (), s32[]{:S(2)}) async-start(), calls=%async_computation.2 | async-start | bytes 131072 | tf_op jit(solution)/shard_map/psum | solution.py:52
  140.0 261.8 %all-gather.5.cloned.1.call-start = ((), (), s32[]{:S(2)}) async-start(), calls=%async_computation.1 | async-start | bytes 16908288 | tf_op jit(solution)/shard_map/all_gather | solution.py:11
  140.8 485.0 %all-reduce.5.cloned.1.call-start = ((), (), s32[]{:S(2)}) async-start(), calls=%async_computation.3 | async-start | bytes 131072 | tf_op jit(solution)/shard_map/psum | solution.py:56
Sparse Core Ops, SparseCore 0:
  11.7 83.9 all-gather.2
  140.1 179.2 all-reduce.2
  323.7 78.0 all-gather.4
  446.6 179.2 all-reduce.4
where the time goes:
time: 661 us; the launch traced here: 659 us
  waiting for transfers between devices  501 us (76%)
  other arithmetic  57.6 us (9%)
  local copies, waits for them, and re-layouts  53.2 us (8%)
  matrix products  32.1 us (5%)
  between operations  14.5 us (2%)
    psum x1, waiting for transfers between devices, local(): second_gram = lax.psum(local_gram(second, item_total), ('hst', 'chip'))  179 us
    psum x1, waiting for transfers between devices, local(): first_gram = lax.psum(local_gram(first_image, item_total), ('hst', 'chip'))  179 us
    all_gather x2, waiting for transfers between devices, fetch_basis(): return lax.all_gather(scaled, ('hst', 'chip'), axis=0, tiled=True)  143 us
    gather x8, local copies, waits for them, and re-layouts, add_group(): picked = blocks[columns]  51.3 us
    another operation x6, other arithmetic, factor_inverse(): lower_factor = jnp.linalg.cholesky(gram_matrix)  24.8 us
    another operation x4, other arithmetic, factor_inverse(): lax.linalg.triangular_solve(lower_factor, identity, left_side=True, lower...  21.6 us
    dot_general x8, matrix products, add_group(): jnp.einsum('sij,sjk->sik', tile_part, picked, preferred_element_type=jnp....  18.4 us
  transfers between devices with their start and end apart: 4, of which 4 were waited for; matrix products, arithmetic and copies ran while one was open for 4% of the time, Pallas kernels for 0%

commit v1 on v0

v1 whole, which is shorter than its diff:
```python
import functools

import jax
import jax.numpy as jnp
from jax import lax
from jax.experimental import pallas as pl
from jax.experimental.pallas import tpu as pltpu
from jax.sharding import PartitionSpec as P

BLK = 512
K = 128
SLOTS = 32
RING = 4
WAVES = 2
DEPTH = BLK // WAVES
MESH = pl.DeviceIdType.MESH
HIGHEST = lax.Precision.HIGHEST
ALL = pl.ds(0, RING)
HALVES = ((1, pl.ds(0, 2)), (3, pl.ds(2, 2)))
ORDER = ((1, 0, 2), (0, 2, 1), (2, 1, 0))
ROWS = (((0, 96), (96, 80), (176, 80)), ((0, 80), (80, 80), (160, 96)))
GRAM_ROWS = ((0, 24), (24, 24), (48, 16))
COPIES = 280
SUMS = 40


def position():
    host, chip = lax.axis_index("hst"), lax.axis_index("chip")
    return (host // RING, lax.rem(host, RING), chip // 2), lax.rem(chip, 2)


class Links:
    def __init__(self, send, recv):
        self.send, self.recv = send, recv
        self.pos, self.core = position()
        self.ids, self.started = {}, []

    def at(self, axis, delta):
        return lax.rem(self.pos[axis] + delta, RING)

    def device(self, axis=None, delta=0):
        place = list(self.pos)
        core = self.core
        if axis is None:
            core = 1 - core
        else:
            place[axis] = self.at(axis, delta)
        return (place[0] * RING + place[1], place[2] * 2 + core)

    def copy(self, key, src, dst, device):
        index = self.ids.setdefault(key, len(self.ids))
        return pltpu.make_async_remote_copy(
            src_ref=src,
            dst_ref=dst,
            send_sem=self.send.at[index],
            recv_sem=self.recv.at[index],
            device_id=device,
            device_id_type=MESH,
        )

    def start(self, key, src, dst, device):
        copy = self.copy(key, src, dst, device)
        copy.start()
        self.started.append(copy)

    def wait(self, key, dst):
        self.copy(key, dst, dst, self.device()).wait_recv()

    def finish(self):
        for copy in self.started:
            copy.wait_send()
        self.started = []


class Gather(Links):
    def __init__(self, waves, send, recv):
        super().__init__(send, recv)
        self.waves = waves

    def view(self, w, t, axes, core=None):
        first, rows = ROWS[w][t]
        index = [axes.get(axis, self.pos[axis]) for axis in range(3)]
        core = self.core if core is None else core
        return self.waves[w].at[index[0], index[1], index[2], core, pl.ds(first, rows), :]

    def push(self, key, view, device):
        self.start(key, view, view, device)

    def line(self, t, second=None, third=None, half=ALL):
        axes = {ORDER[t][0]: half}
        if second is not None:
            axes[ORDER[t][1]] = second
        if third is not None:
            axes[ORDER[t][2]] = third
        return axes

    def seconds(self, t):
        return [self.at(ORDER[t][1], delta) for delta in (0, 3, 1, 2)]

    def first_start(self, w, t):
        for delta in (1, 3, 2):
            self.push((w, t, 1, delta), self.view(w, t, {}), self.device(ORDER[t][0], delta))

    def third_line(self, w, t, j):
        view = self.view(w, t, self.line(t, self.seconds(t)[j]))
        for delta in (1, 3):
            self.push((w, t, 3, delta, j), view, self.device(ORDER[t][2], delta))
        self.sibling(w, t, j, 0)

    def sibling(self, w, t, j, away):
        axes = self.line(t, self.seconds(t)[j], self.at(ORDER[t][2], 4 - away))
        self.push((w, t, "s", j, away), self.view(w, t, axes), self.device())

    def first_end(self, w, t):
        axis = ORDER[t][0]
        for delta in (1, 3, 2):
            self.wait((w, t, 1, delta), self.view(w, t, {axis: self.at(axis, 4 - delta)}))
        view = self.view(w, t, self.line(t))
        for delta in (1, 3):
            self.push((w, t, 2, delta), view, self.device(ORDER[t][1], delta))
        self.third_line(w, t, 0)

    def second_pass(self, w, t, k):
        delta, half = HALVES[k]
        source = self.seconds(t)[k + 1]
        self.wait((w, t, 2, delta), self.view(w, t, self.line(t, source)))
        view = self.view(w, t, self.line(t, source, half=half))
        self.push((w, t, 2, delta, "f"), view, self.device(ORDER[t][1], delta))
        self.third_line(w, t, k + 1)

    def second_end(self, w, t):
        source = self.seconds(t)[3]
        for delta, half in HALVES:
            self.wait((w, t, 2, delta, "f"), self.view(w, t, self.line(t, source, half=half)))
        self.third_line(w, t, 3)

    def third_pass(self, w, t, j):
        axis, source = ORDER[t][2], self.seconds(t)[j]
        for delta, half in HALVES:
            origin = self.at(axis, 4 - delta)
            self.wait((w, t, 3, delta, j), self.view(w, t, self.line(t, source, origin)))
            view = self.view(w, t, self.line(t, source, origin, half=half))
            self.push((w, t, 3, delta, j, "f"), view, self.device(axis, delta))
            self.sibling(w, t, j, delta)

    def third_end(self, w, t, j):
        axis, source = ORDER[t][2], self.seconds(t)[j]
        for delta, half in HALVES:
            view = self.view(w, t, self.line(t, source, self.at(axis, 2), half=half))
            self.wait((w, t, 3, delta, j, "f"), view)
        self.sibling(w, t, j, 2)

    def sibling_end(self, w):
        for t in range(3):
            for j in range(4):
                for away in range(4):
                    axes = self.line(t, self.seconds(t)[j], self.at(ORDER[t][2], 4 - away))
                    self.wait((w, t, "s", j, away), self.view(w, t, axes, core=1 - self.core))

    def events(self):
        plan = [(self.first_start,), (self.first_end,), (self.second_pass, 0), (self.second_pass, 1)]
        plan += [(self.second_end,), (self.third_pass, 0), (self.third_pass, 1), (self.third_end, 0)]
        plan += [(self.third_pass, 2), (self.third_end, 1), (self.third_pass, 3), (self.third_end, 2)]
        plan += [(self.third_end, 3)]
        for step, *more in plan:
            for w in range(WAVES):
                for t in range(3):
                    yield functools.partial(step, w, t, *more)


class Sum(Links):
    def __init__(self, sibling_half, stages, total, send, recv):
        super().__init__(send, recv)
        self.sibling_half, self.stages, self.total = sibling_half, stages, total
        self.half = K // 2

    def rows(self, core):
        return pl.ds(pl.multiple_of(core * self.half, self.half), self.half)

    def begin(self, matrix):
        self.matrix = matrix
        self.start("s", matrix.at[self.rows(1 - self.core)], self.sibling_half, self.device())

    def stage_start(self, stage, value):
        for t in range(3):
            first, rows = GRAM_ROWS[t]
            axis = ORDER[t][stage]
            own = self.stages.at[stage, self.pos[axis], pl.ds(first, rows)]
            own[...] = value[first : first + rows]
            for delta in (2, 1, 3):
                self.push((stage, t, delta), own, self.device(axis, delta))

    def push(self, key, view, device):
        self.start(key, view, view, device)

    def stage_end(self, stage):
        parts = []
        for t in range(3):
            first, rows = GRAM_ROWS[t]
            axis = ORDER[t][stage]
            for delta in (1, 3, 2):
                view = self.stages.at[stage, self.at(axis, 4 - delta), pl.ds(first, rows)]
                self.wait((stage, t, delta), view)
            slots = [self.stages[stage, p, first : first + rows] for p in range(RING)]
            parts.append((slots[0] + slots[1]) + (slots[2] + slots[3]))
        return jnp.concatenate(parts, axis=0)

    def step_one(self):
        self.wait("s", self.sibling_half)
        self.stage_start(0, self.matrix[self.rows(self.core)] + self.sibling_half[...])

    def step_two(self):
        self.stage_start(1, self.stage_end(0))

    def step_three(self):
        self.stage_start(2, self.stage_end(1))

    def step_four(self):
        mine = self.total.at[self.rows(self.core)]
        mine[...] = self.stage_end(2)
        self.start("e", mine, mine, self.device())

    def step_five(self):
        self.wait("e", self.total.at[self.rows(1 - self.core)])


def product(left, right, left_dim, right_dim):
    dims = (((left_dim,), (right_dim,)), ((), ()))
    return lax.dot_general(left, right, dims, precision=HIGHEST, preferred_element_type=jnp.float32)


def factor_inverse(matrix, panel=32, pivots=8):
    ids = [lax.broadcasted_iota(jnp.int32, (K, K), dim) for dim in (0, 1)]
    side = jnp.where(ids[0] == ids[1], 1.0, 0.0)
    row = lax.broadcasted_iota(jnp.int32, (panel, K), 0)
    lane = lax.broadcasted_iota(jnp.int32, (panel, K), 1)
    uppers, inverses = [], []
    for first in range(0, K, panel):
        a, w = matrix[:panel], side[:panel]
        for j in range(0, panel, pivots):
            span = range(pivots)
            cols = [
                jnp.broadcast_to(a[:, first + j + q : first + j + q + 1], (panel, K)) for q in span
            ]
            row_a = [a[j + q : j + q + 1] for q in span]
            row_w = [w[j + q : j + q + 1] for q in span]
            small = [[cols[k][j + q : j + q + 1] for k in span] for q in span]
            for q in span:
                inverse = 1.0 / small[q][q]
                ratio = {k: small[q][k] * inverse for k in range(q + 1, pivots)}
                for k in range(q + 1, pivots):
                    for m in range(k, pivots):
                        small[k][m] = small[k][m] - ratio[k] * small[q][m]
                    row_a[k] = row_a[k] - ratio[k] * row_a[q]
                    row_w[k] = row_w[k] - ratio[k] * row_w[q]
                weight = jnp.where(row > j + q, cols[q], 0.0) * inverse
                for k in range(q + 1, pivots):
                    cols[k] = cols[k] - cols[q] * ratio[k]
                a = a - weight * row_a[q]
                w = w - weight * row_w[q]
        diagonal = jnp.sum(jnp.where(lane == row + first, a, 0.0), axis=1, keepdims=True)
        scale = lax.rsqrt(diagonal)
        a = jnp.where(lane >= row + first, a * scale, 0.0)
        w = w * scale
        uppers.append(a)
        inverses.append(w)
        if first + panel < K:
            rest = a[:, first + panel :]
            matrix = matrix[panel:] - product(rest, a, 0, 0)
            side = side[panel:] - product(rest, w, 0, 0)
    return jnp.concatenate(uppers, axis=0), jnp.concatenate(inverses, axis=0)


def kernel(
    cols,
    live,
    tiles_hbm,
    degree,
    basis,
    leading,
    factor,
    tiles,
    a0,
    a1,
    b0,
    b1,
    scale,
    total,
    gram,
    inverse,
    half_one,
    stages_one,
    sum_one,
    half_two,
    stages_two,
    sum_two,
    tile_sem,
    send_a,
    recv_a,
    send_b,
    recv_b,
    send_g,
    recv_g,
    send_h,
    recv_h,
):
    items = float(BLK * 2 * RING**3)
    loads = [
        pltpu.make_async_copy(
            tiles_hbm.at[pl.ds(8 * i, 8)], tiles.at[pl.ds(8 * i, 8)], tile_sem.at[i]
        )
        for i in range(4)
    ]
    first = Gather((a0, a1), send_a, recv_a)
    second = Gather((b0, b1), send_b, recv_b)
    gram_one = Sum(half_one, stages_one, sum_one, send_g, recv_g)
    gram_two = Sum(half_two, stages_two, sum_two, send_h, recv_h)
    pos, core = first.pos, first.core

    barrier = pltpu.get_barrier_semaphore()
    near = [first.device()] + [first.device(axis, d) for axis in range(3) for d in (1, 2, 3)]
    for device in near:
        pl.semaphore_signal(barrier, inc=1, device_id=device, device_id_type=MESH)
    for load in loads:
        load.start()

    for i in range(BLK // K):
        row_scale = 1.0 / jnp.sqrt(degree[pl.ds(i * K, K)].astype(jnp.float32))
        scale[pl.ds(i * K, K)] = jnp.broadcast_to(row_scale.reshape(1, K), (K, K)).T

    def place(waves, w, value):
        waves[w][pos[0], pos[1], pos[2], core] = value.astype(jnp.bfloat16)

    for w in range(WAVES):
        rows = pl.ds(w * DEPTH, DEPTH)
        place((a0, a1), w, scale[rows] * basis[rows].astype(jnp.float32))
    pl.semaphore_wait(barrier, len(near))

    def multiply(wave, w):
        depth = pl.ds(w * DEPTH, DEPTH)
        if w == 0:
            total[...] = jnp.zeros_like(total)

        @pl.loop(0, SLOTS // 4)
        def _(group):
            parts = []
            for u in range(4):
                slot = group * 4 + u
                col = cols[slot]
                picked = wave[col // 32, lax.rem(col // 8, 4), lax.rem(col // 2, 4), lax.rem(col, 2)]
                picked = jnp.where(slot < live[0], picked, jnp.zeros_like(picked))
                parts.append(
                    jnp.dot(tiles[slot, :, depth], picked, preferred_element_type=jnp.float32)
                )
            total[...] += (parts[0] + parts[1]) + (parts[2] + parts[3])

    for event in first.events():
        event()
    for load in loads:
        load.wait()
    for w in range(WAVES):
        first.sibling_end(w)
        multiply((a0, a1)[w], w)
    for w in range(WAVES):
        rows = pl.ds(w * DEPTH, DEPTH)
        image = total[rows] * scale[rows]
        total[rows] = image
        place((b0, b1), w, scale[rows] * image)

    events = list(second.events())
    for event in events[:12]:
        event()
    image = total[...]
    gram[...] = product(image, image, 0, 0) * (1.0 / items)
    gram_one.begin(gram)
    for event in events[12:24]:
        event()
    gram_one.step_one()
    for event in events[24:30]:
        event()
    gram_one.step_two()
    for event in events[30:36]:
        event()
    gram_one.step_three()
    for event in events[36:42]:
        event()
    gram_one.step_four()
    for event in events[42:48]:
        event()
    gram_one.step_five()
    _, inverse[...] = factor_inverse(sum_one[...])
    for event in events[48:]:
        event()
    for w in range(WAVES):
        second.sibling_end(w)
        multiply((b0, b1)[w], w)
    raw = total[...] * scale[...]
    image = product(raw, inverse[...], 1, 1)
    total[...] = image
    gram_one.finish()
    gram[...] = product(image, image, 0, 0) * (1.0 / items)
    gram_two.begin(gram)
    gram_two.step_one()
    gram_two.step_two()
    gram_two.step_three()
    gram_two.step_four()
    gram_two.step_five()
    upper, inverse[...] = factor_inverse(sum_two[...])
    factor[...] = upper.T
    leading[...] = product(total[...], inverse[...], 1, 1)
    first.finish()
    second.finish()
    gram_two.finish()


def local(tile_data, tile_col, live_count, degree, start_basis):
    vmem, smem = pl.BlockSpec(memory_space=pltpu.VMEM), pl.BlockSpec(memory_space=pltpu.SMEM)
    wave = pltpu.VMEM((RING, RING, RING, 2, DEPTH, K), jnp.bfloat16)
    sums = [
        pltpu.VMEM((K // 2, K), jnp.float32),
        pltpu.VMEM((3, RING, K // 2, K), jnp.float32),
        pltpu.VMEM((K, K), jnp.float32),
    ]
    dma = pltpu.SemaphoreType.DMA
    return pl.pallas_call(
        kernel,
        out_shape=(
            jax.ShapeDtypeStruct((BLK, K), jnp.float32),
            jax.ShapeDtypeStruct((K, K), jnp.float32),
        ),
        in_specs=[smem, smem, pl.BlockSpec(memory_space=pl.ANY), vmem, vmem],
        out_specs=(vmem, vmem),
        scratch_shapes=[
            pltpu.VMEM((SLOTS, BLK, BLK), jnp.bfloat16),
            wave,
            wave,
            wave,
            wave,
            pltpu.VMEM((BLK, K), jnp.float32),
            pltpu.VMEM((BLK, K), jnp.float32),
            pltpu.VMEM((K, K), jnp.float32),
            pltpu.VMEM((K, K), jnp.float32),
            *sums,
            *sums,
            dma((4,)),
            dma((COPIES,)),
            dma((COPIES,)),
            dma((COPIES,)),
            dma((COPIES,)),
            dma((SUMS,)),
            dma((SUMS,)),
            dma((SUMS,)),
            dma((SUMS,)),
        ],
        compiler_params=pltpu.CompilerParams(
            collective_id=0, has_side_effects=True, vmem_limit_bytes=58 * 2**20
        ),
        name="subspace_iteration",
    )(tile_col, live_count, tile_data, degree, start_basis)


def solution(mesh):
    placed = (
        P(("hst", "chip"), None, None),
        P(("hst", "chip")),
        P(("hst", "chip")),
        P(("hst", "chip")),
        P(("hst", "chip"), None),
    )
    return jax.shard_map(
        local,
        mesh=mesh,
        in_specs=placed,
        out_specs=(P(("hst", "chip"), None), P()),
        check_vma=False,
    )
```

time: 661 us -> 142 us (0.21)
  waiting for transfers between devices: 501 us -> 0 us
  Pallas kernels: 0 us -> 137 us
  other arithmetic: 57.6 us -> 0 us
  local copies, waits for them, and re-layouts: 53.2 us -> 3.14 us
  matrix products: 32.1 us -> 0 us
  between operations: 14.5 us -> 1.29 us
    psum x2 -> x0, waiting for transfers between devices: 358 us -> none  [the longest x1 179 us: local(): second_gram = lax.psum(local_gram(second, item_total), ('hst', 'chip'))]
    all_gather x2 -> x0, waiting for transfers between devices: 143 us -> none  [fetch_basis(): return lax.all_gather(scaled, ('hst', 'chip'), axis=0, tiled=True)]
    pallas_call x0 -> x1, Pallas kernels: none -> 137 us  [local(): pl.pallas_call(kernel, out_shape=(jax.ShapeDtypeStruct((BLK, K), jnp.floa...]
    gather x8 -> x0, local copies, waits for them, and re-layouts: 51.3 us -> none  [add_group(): picked = blocks[columns]]
    another operation x10 -> x0, other arithmetic: 46.3 us -> none  [the longest x6 24.8 us: factor_inverse(): lower_factor = jnp.linalg.cholesky(gram_matrix)]
    dot_general x20 -> x0, matrix products: 31.6 us -> none  [the longest x8 18.4 us: add_group(): jnp.einsum('sij,sjk->sik', tile_part, picked, preferred_element_type=jnp....]
  transfers between devices with their start and end apart: 4 -> 0, of which waited for: 4 -> 0; matrix products, arithmetic and copies ran while one was open for 4% -> 0% of each run, Pallas kernels for 0% -> 0%
where the time goes in v1:
time: 142 us
  Pallas kernels  137 us (96%)
  local copies, waits for them, and re-layouts  3.14 us (2%)
    pallas_call x1, Pallas kernels, local(): pl.pallas_call(kernel, out_shape=(jax.ShapeDtypeStruct((BLK, K), jnp.floa...  137 us
    unnamed x2, local copies, waits for them, and re-layouts  3.14 us

profile of v1, /device:TPU:1, one launch (start us, length us, event | category | flops | bytes accessed | tf_op | source)
XLA Modules:
  0.0 141.7 jit_solution(5187230720560707576)
XLA Ops:
  1.3 137.3 %subspace_iteration.1 = (f32[512,128]{1,0:T(8,128)}, f32[128,128]{1,0:T(8,128)}) custom-call(s32[32]{0:T(128)} %cols.1, s32[1]{0:T(128)S(6)} %copy.9.live, bf16[32,512,512]{2,1,0:T(8,128)(2,1)} %tiles_hbm.1, s32[512]{0:T(512)} %degree.1, bf16[512,128]{1,0:T(8,128)(2,1)} %basis.1), custom_call_target="tpu_custom_call" | custom-call | tf_op jit(solution)/shard_map/subspace_iteration/pallas_call | solution.py:425
  138.5 1.7 %copy.10 = f32[512,128]{1,0:T(8,128)} copy(f32[512,128]{1,0:T(8,128)} %get-tuple-element.4) | data formatting | bytes 524288
  140.2 1.5 %copy.11 = f32[128,128]{1,0:T(8,128)} copy(f32[128,128]{1,0:T(8,128)} %get-tuple-element.5) | data formatting | bytes 131072

commit v2 on v1

--- a/solution.py
+++ b/solution.py
@@ -20,8 +20,31 @@
 ORDER = ((1, 0, 2), (0, 2, 1), (2, 1, 0))
 ROWS = (((0, 96), (96, 80), (176, 80)), ((0, 80), (80, 80), (160, 96)))
 GRAM_ROWS = ((0, 24), (24, 24), (48, 16))
-COPIES = 280
+COPIES = 240
 SUMS = 40
+GROUP = 16
+WHOLE_ONE = ((False, False, False), (True, True, False))
+WHOLE_TWO = ((False, False, False), (True, True, False))
+ROUND_ONE = (
+    ("first", 1), ("first", 0), ("line", 1), ("line", 0), ("plane", 1, 0), ("plane", 0, 0),
+    ("plane", 0, 1), ("plane", 1, 1), ("planed", 0), ("pass", 0, 0), ("share", 0, 0),
+    ("pass", 0, 1), ("pass", 0, 2), ("pass", 0, 3), ("planed", 1), ("pass", 1, 0), ("far", 0, 0),
+    ("far", 0, 1), ("pass", 1, 1), ("pass", 1, 2), ("share", 0, 1), ("far", 0, 2), ("far", 0, 3),
+    ("share", 1, 0), ("share", 0, 3), ("share", 0, 2), ("pass", 1, 3), ("loaded",),
+    ("multiply", 0, 0, 1), ("far", 1, 0), ("far", 1, 1), ("multiply", 0, 1, 2), ("far", 1, 2),
+    ("far", 1, 3), ("share", 1, 1), ("share", 1, 3), ("share", 1, 2),
+)
+ROUND_TWO = (
+    ("first", 0), ("half",), ("first", 1), ("line", 0), ("gram",), ("sum", 0), ("line", 1),
+    ("sum", 1), ("plane", 0, 0), ("plane", 0, 1), ("sum", 2), ("plane", 1, 0), ("plane", 1, 1),
+    ("planed", 0), ("pass", 0, 0), ("sum", 3), ("pass", 0, 1), ("pass", 0, 2), ("sum", 4),
+    ("eliminate", 0), ("eliminate", 1), ("eliminate", 2), ("eliminate", 3), ("pass", 0, 3),
+    ("planed", 1), ("share", 0, 0), ("pass", 1, 0), ("far", 0, 0), ("pass", 1, 1), ("far", 0, 1),
+    ("share", 0, 1), ("far", 0, 2), ("far", 0, 3), ("share", 0, 3), ("pass", 1, 2), ("share", 0, 2),
+    ("pass", 1, 3), ("multiply", 0, 0, 1), ("far", 1, 0), ("far", 1, 1), ("multiply", 0, 1, 2),
+    ("far", 1, 2), ("far", 1, 3), ("share", 1, 0), ("share", 1, 1), ("share", 1, 3),
+    ("share", 1, 2), ("multiply", 1, 0, 2),
+)
 
 
 def position():
@@ -73,9 +96,9 @@
 
 
 class Gather(Links):
-    def __init__(self, waves, send, recv):
+    def __init__(self, waves, send, recv, whole):
         super().__init__(send, recv)
-        self.waves = waves
+        self.waves, self.whole = waves, whole
 
     def view(self, w, t, axes, core=None):
         first, rows = ROWS[w][t]
@@ -107,9 +130,21 @@
             self.push((w, t, 3, delta, j), view, self.device(ORDER[t][2], delta))
         self.sibling(w, t, j, 0)
 
+    def shared(self, w, t, j, away):
+        if self.whole[w][(0, 1, 2, 1)[away]]:
+            return self.line(t, ALL, self.at(ORDER[t][2], 4 - away)) if j == 3 else None
+        return self.line(t, self.seconds(t)[j], self.at(ORDER[t][2], 4 - away))
+
     def sibling(self, w, t, j, away):
-        axes = self.line(t, self.seconds(t)[j], self.at(ORDER[t][2], 4 - away))
-        self.push((w, t, "s", j, away), self.view(w, t, axes), self.device())
+        axes = self.shared(w, t, j, away)
+        if axes is not None:
+            self.push((w, t, "s", j, away), self.view(w, t, axes), self.device())
+
+    def sibling_end(self, w, t, away):
+        for j in range(4):
+            axes = self.shared(w, t, j, away)
+            if axes is not None:
+                self.wait((w, t, "s", j, away), self.view(w, t, axes, core=1 - self.core))
 
     def first_end(self, w, t):
         axis = ORDER[t][0]
@@ -150,22 +185,18 @@
             self.wait((w, t, 3, delta, j, "f"), view)
         self.sibling(w, t, j, 2)
 
-    def sibling_end(self, w):
+    def take(self, name, w, *more):
+        step = {
+            "first": self.first_start,
+            "line": self.first_end,
+            "plane": self.second_pass,
+            "planed": self.second_end,
+            "pass": self.third_pass,
+            "far": self.third_end,
+            "share": self.sibling_end,
+        }[name]
         for t in range(3):
-            for j in range(4):
-                for away in range(4):
-                    axes = self.line(t, self.seconds(t)[j], self.at(ORDER[t][2], 4 - away))
-                    self.wait((w, t, "s", j, away), self.view(w, t, axes, core=1 - self.core))
-
-    def events(self):
-        plan = [(self.first_start,), (self.first_end,), (self.second_pass, 0), (self.second_pass, 1)]
-        plan += [(self.second_end,), (self.third_pass, 0), (self.third_pass, 1), (self.third_end, 0)]
-        plan += [(self.third_pass, 2), (self.third_end, 1), (self.third_pass, 3), (self.third_end, 2)]
-        plan += [(self.third_end, 3)]
-        for step, *more in plan:
-            for w in range(WAVES):
-                for t in range(3):
-                    yield functools.partial(step, w, t, *more)
+            step(w, t, *more)
 
 
 class Sum(Links):
@@ -205,6 +236,9 @@
             parts.append((slots[0] + slots[1]) + (slots[2] + slots[3]))
         return jnp.concatenate(parts, axis=0)
 
+    def take(self, step):
+        (self.step_one, self.step_two, self.step_three, self.step_four, self.step_five)[step]()
+
     def step_one(self):
         self.wait("s", self.sibling_half)
         self.stage_start(0, self.matrix[self.rows(self.core)] + self.sibling_half[...])
@@ -229,7 +263,7 @@
     return lax.dot_general(left, right, dims, precision=HIGHEST, preferred_element_type=jnp.float32)
 
 
-def factor_inverse(matrix, panel=32, pivots=8):
+def factor_inverse(matrix, result, panel=32, pivots=8):
     ids = [lax.broadcasted_iota(jnp.int32, (K, K), dim) for dim in (0, 1)]
     side = jnp.where(ids[0] == ids[1], 1.0, 0.0)
     row = lax.broadcasted_iota(jnp.int32, (panel, K), 0)
@@ -268,17 +302,22 @@
             rest = a[:, first + panel :]
             matrix = matrix[panel:] - product(rest, a, 0, 0)
             side = side[panel:] - product(rest, w, 0, 0)
-    return jnp.concatenate(uppers, axis=0), jnp.concatenate(inverses, axis=0)
+        yield
+    result.extend((jnp.concatenate(uppers, axis=0), jnp.concatenate(inverses, axis=0)))
 
 
 def kernel(
+    cols_hbm,
+    live_hbm,
+    tiles_hbm,
+    degree_hbm,
+    basis_hbm,
+    image_hbm,
+    sum_hbm,
     cols,
     live,
-    tiles_hbm,
     degree,
     basis,
-    leading,
-    factor,
     tiles,
     a0,
     a1,
@@ -287,14 +326,13 @@
     scale,
     total,
     gram,
-    inverse,
     half_one,
     stages_one,
     sum_one,
     half_two,
     stages_two,
     sum_two,
-    tile_sem,
+    load_sem,
     send_a,
     recv_a,
     send_b,
@@ -305,14 +343,8 @@
     recv_h,
 ):
     items = float(BLK * 2 * RING**3)
-    loads = [
-        pltpu.make_async_copy(
-            tiles_hbm.at[pl.ds(8 * i, 8)], tiles.at[pl.ds(8 * i, 8)], tile_sem.at[i]
-        )
-        for i in range(4)
-    ]
-    first = Gather((a0, a1), send_a, recv_a)
-    second = Gather((b0, b1), send_b, recv_b)
+    first = Gather((a0, a1), send_a, recv_a, WHOLE_ONE)
+    second = Gather((b0, b1), send_b, recv_b, WHOLE_TWO)
     gram_one = Sum(half_one, stages_one, sum_one, send_g, recv_g)
     gram_two = Sum(half_two, stages_two, sum_two, send_h, recv_h)
     pos, core = first.pos, first.core
@@ -321,100 +353,110 @@
     near = [first.device()] + [first.device(axis, d) for axis in range(3) for d in (1, 2, 3)]
     for device in near:
         pl.semaphore_signal(barrier, inc=1, device_id=device, device_id_type=MESH)
+    pairs = [(degree_hbm, degree), (basis_hbm, basis), (cols_hbm, cols), (live_hbm, live)]
+    pairs += [(tiles_hbm.at[pl.ds(8 * i, 8)], tiles.at[pl.ds(8 * i, 8)]) for i in range(4)]
+    loads = [pltpu.make_async_copy(*pair, load_sem.at[i]) for i, pair in enumerate(pairs)]
     for load in loads:
         load.start()
 
+    def place(waves, w, value):
+        waves[w][pos[0], pos[1], pos[2], core] = value.astype(jnp.bfloat16)
+
+    loads[0].wait()
     for i in range(BLK // K):
         row_scale = 1.0 / jnp.sqrt(degree[pl.ds(i * K, K)].astype(jnp.float32))
         scale[pl.ds(i * K, K)] = jnp.broadcast_to(row_scale.reshape(1, K), (K, K)).T
-
-    def place(waves, w, value):
-        waves[w][pos[0], pos[1], pos[2], core] = value.astype(jnp.bfloat16)
-
+    loads[1].wait()
     for w in range(WAVES):
         rows = pl.ds(w * DEPTH, DEPTH)
         place((a0, a1), w, scale[rows] * basis[rows].astype(jnp.float32))
     pl.semaphore_wait(barrier, len(near))
 
-    def multiply(wave, w):
-        depth = pl.ds(w * DEPTH, DEPTH)
-        if w == 0:
-            total[...] = jnp.zeros_like(total)
-
-        @pl.loop(0, SLOTS // 4)
+    def multiply(waves, w, groups, rows=pl.ds(0, BLK)):
+        @pl.loop(*groups)
         def _(group):
             parts = []
-            for u in range(4):
-                slot = group * 4 + u
+            for u in range(GROUP):
+                slot = group * GROUP + u
                 col = cols[slot]
-                picked = wave[col // 32, lax.rem(col // 8, 4), lax.rem(col // 2, 4), lax.rem(col, 2)]
+                picked = waves[w][
+                    col // 32, lax.rem(col // 8, 4), lax.rem(col // 2, 4), lax.rem(col, 2)
+                ]
                 picked = jnp.where(slot < live[0], picked, jnp.zeros_like(picked))
-                parts.append(
-                    jnp.dot(tiles[slot, :, depth], picked, preferred_element_type=jnp.float32)
-                )
-            total[...] += (parts[0] + parts[1]) + (parts[2] + parts[3])
-
-    for event in first.events():
-        event()
-    for load in loads:
-        load.wait()
-    for w in range(WAVES):
-        first.sibling_end(w)
-        multiply((a0, a1)[w], w)
-    for w in range(WAVES):
+                tile = tiles[slot, rows, pl.ds(w * DEPTH, DEPTH)]
+                parts.append(jnp.dot(tile, picked, preferred_element_type=jnp.float32))
+            while len(parts) > 1:
+                parts = [left + right for left, right in zip(parts[::2], parts[1::2])]
+            total[rows] += parts[0]
+
+    total[...] = jnp.zeros_like(total)
+    for name, *more in ROUND_ONE:
+        if name == "multiply":
+            multiply(first.waves, more[0], more[1:])
+        elif name == "loaded":
+            for load in loads[2:]:
+                load.wait()
+        else:
+            first.take(name, *more)
+
+    def half_image(w):
         rows = pl.ds(w * DEPTH, DEPTH)
+        multiply(first.waves, 1, (0, SLOTS // GROUP), rows)
         image = total[rows] * scale[rows]
         total[rows] = image
         place((b0, b1), w, scale[rows] * image)
 
-    events = list(second.events())
-    for event in events[:12]:
-        event()
-    image = total[...]
-    gram[...] = product(image, image, 0, 0) * (1.0 / items)
-    gram_one.begin(gram)
-    for event in events[12:24]:
-        event()
-    gram_one.step_one()
-    for event in events[24:30]:
-        event()
-    gram_one.step_two()
-    for event in events[30:36]:
-        event()
-    gram_one.step_three()
-    for event in events[36:42]:
-        event()
-    gram_one.step_four()
-    for event in events[42:48]:
-        event()
-    gram_one.step_five()
-    _, inverse[...] = factor_inverse(sum_one[...])
-    for event in events[48:]:
-        event()
-    for w in range(WAVES):
-        second.sibling_end(w)
-        multiply((b0, b1)[w], w)
+    factors = []
+    half_image(0)
+    for name, *more in ROUND_TWO:
+        if name == "half":
+            half_image(1)
+        elif name == "gram":
+            image = total[...]
+            total[...] = jnp.zeros_like(total)
+            gram[...] = product(image, image, 0, 0) * (1.0 / items)
+            gram_one.begin(gram)
+        elif name == "sum":
+            gram_one.take(more[0])
+        elif name == "eliminate":
+            if more[0] == 0:
+                elimination = factor_inverse(sum_one[...], factors)
+            next(elimination)
+        elif name == "multiply":
+            multiply(second.waves, more[0], more[1:])
+        else:
+            second.take(name, *more)
+    next(elimination, None)
     raw = total[...] * scale[...]
-    image = product(raw, inverse[...], 1, 1)
+    image = product(raw, factors[1], 1, 1)
     total[...] = image
+    out = pltpu.make_async_copy(total, image_hbm, load_sem.at[0])
+    out.start()
     gram_one.finish()
     gram[...] = product(image, image, 0, 0) * (1.0 / items)
     gram_two.begin(gram)
-    gram_two.step_one()
-    gram_two.step_two()
-    gram_two.step_three()
-    gram_two.step_four()
-    gram_two.step_five()
-    upper, inverse[...] = factor_inverse(sum_two[...])
-    factor[...] = upper.T
-    leading[...] = product(total[...], inverse[...], 1, 1)
+    for step in range(5):
+        gram_two.take(step)
+    out_sum = pltpu.make_async_copy(sum_two, sum_hbm, load_sem.at[1])
+    out_sum.start()
     first.finish()
     second.finish()
     gram_two.finish()
+    out.wait()
+    out_sum.wait()
+
+
+def finish(image, gram, leading, factor):
+    factors = []
+    for _ in factor_inverse(gram[...], factors):
+        pass
+    upper, inverse = factors
+    factor[...] = upper.T
+    leading[...] = product(image[...], inverse, 1, 1)
 
 
 def local(tile_data, tile_col, live_count, degree, start_basis):
-    vmem, smem = pl.BlockSpec(memory_space=pltpu.VMEM), pl.BlockSpec(memory_space=pltpu.SMEM)
+    vmem, anywhere = pl.BlockSpec(memory_space=pltpu.VMEM), pl.BlockSpec(memory_space=pl.ANY)
     wave = pltpu.VMEM((RING, RING, RING, 2, DEPTH, K), jnp.bfloat16)
     sums = [
         pltpu.VMEM((K // 2, K), jnp.float32),
@@ -422,41 +464,40 @@
         pltpu.VMEM((K, K), jnp.float32),
     ]
     dma = pltpu.SemaphoreType.DMA
-    return pl.pallas_call(
+    rows = jax.ShapeDtypeStruct((BLK, K), jnp.float32)
+    square = jax.ShapeDtypeStruct((K, K), jnp.float32)
+    image, gram = pl.pallas_call(
         kernel,
-        out_shape=(
-            jax.ShapeDtypeStruct((BLK, K), jnp.float32),
-            jax.ShapeDtypeStruct((K, K), jnp.float32),
-        ),
-        in_specs=[smem, smem, pl.BlockSpec(memory_space=pl.ANY), vmem, vmem],
-        out_specs=(vmem, vmem),
+        out_shape=(rows, square),
+        in_specs=[anywhere] * 5,
+        out_specs=(anywhere, anywhere),
         scratch_shapes=[
+            pltpu.SMEM((SLOTS,), jnp.int32),
+            pltpu.SMEM((1,), jnp.int32),
+            pltpu.VMEM((BLK,), jnp.int32),
+            pltpu.VMEM((BLK, K), jnp.bfloat16),
             pltpu.VMEM((SLOTS, BLK, BLK), jnp.bfloat16),
-            wave,
-            wave,
-            wave,
-            wave,
+            *[wave] * 4,
             pltpu.VMEM((BLK, K), jnp.float32),
             pltpu.VMEM((BLK, K), jnp.float32),
             pltpu.VMEM((K, K), jnp.float32),
-            pltpu.VMEM((K, K), jnp.float32),
-            *sums,
-            *sums,
-            dma((4,)),
-            dma((COPIES,)),
-            dma((COPIES,)),
-            dma((COPIES,)),
-            dma((COPIES,)),
-            dma((SUMS,)),
-            dma((SUMS,)),
-            dma((SUMS,)),
-            dma((SUMS,)),
+            *sums * 2,
+            dma((8,)),
+            *[dma((COPIES,))] * 4,
+            *[dma((SUMS,))] * 4,
         ],
         compiler_params=pltpu.CompilerParams(
             collective_id=0, has_side_effects=True, vmem_limit_bytes=58 * 2**20
         ),
-        name="subspace_iteration",
+        name="two_rounds",
     )(tile_col, live_count, tile_data, degree, start_basis)
+    return pl.pallas_call(
+        finish,
+        out_shape=(rows, square),
+        in_specs=[vmem] * 2,
+        out_specs=(vmem, vmem),
+        name="finish",
+    )(image, gram)
 
 
 def solution(mesh):

time: 142 us -> 121 us (0.85)
  Pallas kernels: 137 us -> 120 us
  local copies, waits for them, and re-layouts: 3.14 us -> 0 us
    pallas_call x1 -> x2, Pallas kernels: 137 us -> 120 us  [the longest x1 114 us: local(): pl.pallas_call(kernel, out_shape=(rows, square), in_specs=[anywhere] * 5,...]
    unnamed x2 -> x0, local copies, waits for them, and re-layouts: 3.14 us -> none
where the time goes in v2:
time: 121 us
  Pallas kernels  120 us (99%)
  between operations  1.29 us (1%)
    pallas_call x1, Pallas kernels, local(): pl.pallas_call(kernel, out_shape=(rows, square), in_specs=[anywhere] * 5,...  114 us
    pallas_call x1, Pallas kernels, local(): pl.pallas_call(finish, out_shape=(rows, square), in_specs=[vmem] * 2, out...  6.21 us

profile of v2, /device:TPU:1, one launch (start us, length us, event | category | flops | bytes accessed | tf_op | source)
XLA Modules:
  0.0 121.3 jit_solution(1418975541503609617)
XLA Ops:
  1.3 113.8 %two_rounds.1 = (f32[512,128]{1,0:T(8,128)}, f32[128,128]{1,0:T(8,128)}) custom-call(s32[32]{0:T(128)} %cols_hbm.1, s32[1]{0:T(128)S(6)} %copy.7.live_hbm, bf16[32,512,512]{2,1,0:T(8,128)(2,1)} %tiles_hbm.1, s32[512]{0:T(512)} %degree_hbm.1, bf16[512,128]{1,0:T(8,128)(2,1)} %basis_hbm.1), custom_call_target="tpu_custom_call" | custom-call | tf_op jit(solution)/shard_map/two_rounds/pallas_call | solution.py:469
  115.1 6.2 %finish.1 = (f32[512,128]{1,0:T(8,128)}, f32[128,128]{1,0:T(8,128)}) custom-call(f32[512,128]{1,0:T(8,128)} %get-tuple-element.4.image, f32[128,128]{1,0:T(8,128)} %get-tuple-element.5.gram), custom_call_target="tpu_custom_call" | custom-call | tf_op jit(solution)/shard_map/finish/pallas_call | solution.py:494

commit v3 on v2

--- a/solution.py
+++ b/solution.py
@@ -20,30 +20,29 @@
 ORDER = ((1, 0, 2), (0, 2, 1), (2, 1, 0))
 ROWS = (((0, 96), (96, 80), (176, 80)), ((0, 80), (80, 80), (160, 96)))
 GRAM_ROWS = ((0, 24), (24, 24), (48, 16))
-COPIES = 240
-SUMS = 40
+SENDS = 8
+RECEIPTS = 26
+SUMS = 5
 GROUP = 16
-WHOLE_ONE = ((False, False, False), (True, True, False))
-WHOLE_TWO = ((False, False, False), (True, True, False))
+WHOLE_ONE = ((False, False, False), (False, False, False))
+WHOLE_TWO = ((False, False, False), (False, False, False))
 ROUND_ONE = (
-    ("first", 1), ("first", 0), ("line", 1), ("line", 0), ("plane", 1, 0), ("plane", 0, 0),
-    ("plane", 0, 1), ("plane", 1, 1), ("planed", 0), ("pass", 0, 0), ("share", 0, 0),
-    ("pass", 0, 1), ("pass", 0, 2), ("pass", 0, 3), ("planed", 1), ("pass", 1, 0), ("far", 0, 0),
-    ("far", 0, 1), ("pass", 1, 1), ("pass", 1, 2), ("share", 0, 1), ("far", 0, 2), ("far", 0, 3),
-    ("share", 1, 0), ("share", 0, 3), ("share", 0, 2), ("pass", 1, 3), ("loaded",),
+    ("first", 0), ("first", 1), ("line", 0), ("line", 1), ("plane", 0, 0), ("plane", 0, 1),
+    ("plane", 1, 0), ("plane", 1, 1), ("planed", 0), ("pass", 0, 0), ("pass", 0, 1), ("pass", 0, 2),
+    ("pass", 0, 3), ("planed", 1), ("pass", 1, 0), ("far", 0, 0), ("far", 0, 1), ("far", 0, 2),
+    ("pass", 1, 1), ("pass", 1, 2), ("far", 0, 3), ("pass", 1, 3), ("share", 0), ("loaded",),
     ("multiply", 0, 0, 1), ("far", 1, 0), ("far", 1, 1), ("multiply", 0, 1, 2), ("far", 1, 2),
-    ("far", 1, 3), ("share", 1, 1), ("share", 1, 3), ("share", 1, 2),
+    ("far", 1, 3), ("share", 1),
 )
 ROUND_TWO = (
     ("first", 0), ("half",), ("first", 1), ("line", 0), ("gram",), ("sum", 0), ("line", 1),
     ("sum", 1), ("plane", 0, 0), ("plane", 0, 1), ("sum", 2), ("plane", 1, 0), ("plane", 1, 1),
-    ("planed", 0), ("pass", 0, 0), ("sum", 3), ("pass", 0, 1), ("pass", 0, 2), ("sum", 4),
-    ("eliminate", 0), ("eliminate", 1), ("eliminate", 2), ("eliminate", 3), ("pass", 0, 3),
-    ("planed", 1), ("share", 0, 0), ("pass", 1, 0), ("far", 0, 0), ("pass", 1, 1), ("far", 0, 1),
-    ("share", 0, 1), ("far", 0, 2), ("far", 0, 3), ("share", 0, 3), ("pass", 1, 2), ("share", 0, 2),
-    ("pass", 1, 3), ("multiply", 0, 0, 1), ("far", 1, 0), ("far", 1, 1), ("multiply", 0, 1, 2),
-    ("far", 1, 2), ("far", 1, 3), ("share", 1, 0), ("share", 1, 1), ("share", 1, 3),
-    ("share", 1, 2), ("multiply", 1, 0, 2),
+    ("planed", 0), ("sum", 3), ("pass", 0, 0), ("sum", 4), ("eliminate", 0), ("eliminate", 1),
+    ("eliminate", 2), ("pass", 0, 1), ("pass", 0, 2), ("pass", 0, 3), ("planed", 1), ("pass", 1, 0),
+    ("eliminate", 3), ("far", 0, 0), ("pass", 1, 1), ("far", 0, 1), ("far", 0, 2), ("far", 0, 3),
+    ("pass", 1, 2), ("share", 0), ("pass", 1, 3), ("multiply", 0, 0, 1), ("far", 1, 0),
+    ("far", 1, 1), ("multiply", 0, 1, 2), ("far", 1, 2), ("far", 1, 3), ("share", 1),
+    ("multiply", 1, 0, 2),
 )
 
 
@@ -56,7 +55,7 @@
     def __init__(self, send, recv):
         self.send, self.recv = send, recv
         self.pos, self.core = position()
-        self.ids, self.started = {}, []
+        self.send_ids, self.recv_ids = {}, {}
 
     def at(self, axis, delta):
         return lax.rem(self.pos[axis] + delta, RING)
@@ -70,29 +69,21 @@
             place[axis] = self.at(axis, delta)
         return (place[0] * RING + place[1], place[2] * 2 + core)
 
-    def copy(self, key, src, dst, device):
-        index = self.ids.setdefault(key, len(self.ids))
+    def copy(self, out, into, src, dst, device):
         return pltpu.make_async_remote_copy(
             src_ref=src,
             dst_ref=dst,
-            send_sem=self.send.at[index],
-            recv_sem=self.recv.at[index],
+            send_sem=self.send.at[self.send_ids.setdefault(out, len(self.send_ids))],
+            recv_sem=self.recv.at[self.recv_ids.setdefault(into, len(self.recv_ids))],
             device_id=device,
             device_id_type=MESH,
         )
 
-    def start(self, key, src, dst, device):
-        copy = self.copy(key, src, dst, device)
-        copy.start()
-        self.started.append(copy)
-
-    def wait(self, key, dst):
-        self.copy(key, dst, dst, self.device()).wait_recv()
-
-    def finish(self):
-        for copy in self.started:
-            copy.wait_send()
-        self.started = []
+    def wait(self, into, like):
+        self.copy(next(iter(self.send_ids)), into, like, like, self.device()).wait_recv()
+
+    def wait_sent(self, out, like):
+        self.copy(out, next(iter(self.recv_ids)), like, like, self.device()).wait_send()
 
 
 class Gather(Links):
@@ -100,14 +91,17 @@
         super().__init__(send, recv)
         self.waves, self.whole = waves, whole
 
-    def view(self, w, t, axes, core=None):
+    def view(self, w, t, axes):
         first, rows = ROWS[w][t]
         index = [axes.get(axis, self.pos[axis]) for axis in range(3)]
-        core = self.core if core is None else core
-        return self.waves[w].at[index[0], index[1], index[2], core, pl.ds(first, rows), :]
-
-    def push(self, key, view, device):
-        self.start(key, view, view, device)
+        return self.waves[w].at[index[0], index[1], index[2], self.core, pl.ds(first, rows), :]
+
+    def blocks(self, w, y, x, z):
+        return self.waves[w].at[pl.ds(0, y), pl.ds(0, x), pl.ds(0, z), 0]
+
+    def push(self, out, into, w, t, axes, device):
+        view = self.view(w, t, axes)
+        self.copy((w, out), (w, into), view, view, device).start()
 
     def line(self, t, second=None, third=None, half=ALL):
         axes = {ORDER[t][0]: half}
@@ -120,70 +114,68 @@
     def seconds(self, t):
         return [self.at(ORDER[t][1], delta) for delta in (0, 3, 1, 2)]
 
-    def first_start(self, w, t):
-        for delta in (1, 3, 2):
-            self.push((w, t, 1, delta), self.view(w, t, {}), self.device(ORDER[t][0], delta))
+    def first_start(self, w):
+        for t in range(3):
+            for delta in (2, 1, 3):
+                self.push("first", "first", w, t, {}, self.device(ORDER[t][0], delta))
 
     def third_line(self, w, t, j):
-        view = self.view(w, t, self.line(t, self.seconds(t)[j]))
+        axes = self.line(t, self.seconds(t)[j])
         for delta in (1, 3):
-            self.push((w, t, 3, delta, j), view, self.device(ORDER[t][2], delta))
+            self.push("third", ("third", j), w, t, axes, self.device(ORDER[t][2], delta))
         self.sibling(w, t, j, 0)
 
-    def shared(self, w, t, j, away):
-        if self.whole[w][(0, 1, 2, 1)[away]]:
-            return self.line(t, ALL, self.at(ORDER[t][2], 4 - away)) if j == 3 else None
-        return self.line(t, self.seconds(t)[j], self.at(ORDER[t][2], 4 - away))
-
     def sibling(self, w, t, j, away):
-        axes = self.shared(w, t, j, away)
-        if axes is not None:
-            self.push((w, t, "s", j, away), self.view(w, t, axes), self.device())
-
-    def sibling_end(self, w, t, away):
-        for j in range(4):
-            axes = self.shared(w, t, j, away)
-            if axes is not None:
-                self.wait((w, t, "s", j, away), self.view(w, t, axes, core=1 - self.core))
-
-    def first_end(self, w, t):
-        axis = ORDER[t][0]
-        for delta in (1, 3, 2):
-            self.wait((w, t, 1, delta), self.view(w, t, {axis: self.at(axis, 4 - delta)}))
-        view = self.view(w, t, self.line(t))
-        for delta in (1, 3):
-            self.push((w, t, 2, delta), view, self.device(ORDER[t][1], delta))
-        self.third_line(w, t, 0)
-
-    def second_pass(self, w, t, k):
+        third = self.at(ORDER[t][2], 4 - away)
+        if not self.whole[w][(0, 1, 2, 1)[away]]:
+            self.push("share", "share", w, t, self.line(t, self.seconds(t)[j], third), self.device())
+        elif j == 3:
+            self.push("share", "share", w, t, self.line(t, ALL, third), self.device())
+
+    def sibling_end(self, w):
+        self.wait((w, "share"), self.blocks(w, 4, 4, 4))
+
+    def first_end(self, w):
+        self.wait((w, "first"), self.blocks(w, 1, 1, 3))
+        for t in range(3):
+            for delta in (1, 3):
+                device = self.device(ORDER[t][1], delta)
+                self.push("second", ("second", delta), w, t, self.line(t), device)
+            self.third_line(w, t, 0)
+
+    def second_pass(self, w, k):
         delta, half = HALVES[k]
-        source = self.seconds(t)[k + 1]
-        self.wait((w, t, 2, delta), self.view(w, t, self.line(t, source)))
-        view = self.view(w, t, self.line(t, source, half=half))
-        self.push((w, t, 2, delta, "f"), view, self.device(ORDER[t][1], delta))
-        self.third_line(w, t, k + 1)
-
-    def second_end(self, w, t):
-        source = self.seconds(t)[3]
-        for delta, half in HALVES:
-            self.wait((w, t, 2, delta, "f"), self.view(w, t, self.line(t, source, half=half)))
-        self.third_line(w, t, 3)
-
-    def third_pass(self, w, t, j):
-        axis, source = ORDER[t][2], self.seconds(t)[j]
-        for delta, half in HALVES:
-            origin = self.at(axis, 4 - delta)
-            self.wait((w, t, 3, delta, j), self.view(w, t, self.line(t, source, origin)))
-            view = self.view(w, t, self.line(t, source, origin, half=half))
-            self.push((w, t, 3, delta, j, "f"), view, self.device(axis, delta))
-            self.sibling(w, t, j, delta)
-
-    def third_end(self, w, t, j):
-        axis, source = ORDER[t][2], self.seconds(t)[j]
-        for delta, half in HALVES:
-            view = self.view(w, t, self.line(t, source, self.at(axis, 2), half=half))
-            self.wait((w, t, 3, delta, j, "f"), view)
-        self.sibling(w, t, j, 2)
+        self.wait((w, ("second", delta)), self.blocks(w, 1, 1, 4))
+        for t in range(3):
+            axes = self.line(t, self.seconds(t)[k + 1], half=half)
+            self.push("second", "halves", w, t, axes, self.device(ORDER[t][1], delta))
+            self.third_line(w, t, k + 1)
+
+    def second_end(self, w):
+        self.wait((w, "halves"), self.blocks(w, 1, 1, 4))
+        for t in range(3):
+            self.third_line(w, t, 3)
+
+    def third_pass(self, w, j):
+        self.wait((w, ("third", j)), self.blocks(w, 1, 2, 4))
+        for t in range(3):
+            axis, source = ORDER[t][2], self.seconds(t)[j]
+            for delta, half in HALVES:
+                axes = self.line(t, source, self.at(axis, 4 - delta), half)
+                self.push("third", ("far", j), w, t, axes, self.device(axis, delta))
+                self.sibling(w, t, j, delta)
+
+    def third_end(self, w, j):
+        self.wait((w, ("far", j)), self.blocks(w, 1, 1, 4))
+        for t in range(3):
+            self.sibling(w, t, j, 2)
+
+    def finish(self):
+        for w in range(WAVES):
+            self.wait_sent((w, "first"), self.blocks(w, 1, 1, 3))
+            self.wait_sent((w, "second"), self.blocks(w, 1, 3, 4))
+            self.wait_sent((w, "third"), self.blocks(w, 3, 4, 4))
+            self.wait_sent((w, "share"), self.blocks(w, 4, 4, 4))
 
     def take(self, name, w, *more):
         step = {
@@ -195,8 +187,7 @@
             "far": self.third_end,
             "share": self.sibling_end,
         }[name]
-        for t in range(3):
-            step(w, t, *more)
+        step(w, *more)
 
 
 class Sum(Links):
@@ -210,7 +201,8 @@
 
     def begin(self, matrix):
         self.matrix = matrix
-        self.start("s", matrix.at[self.rows(1 - self.core)], self.sibling_half, self.device())
+        out = matrix.at[self.rows(1 - self.core)]
+        self.copy("in", "in", out, self.sibling_half, self.device()).start()
 
     def stage_start(self, stage, value):
         for t in range(3):
@@ -219,43 +211,31 @@
             own = self.stages.at[stage, self.pos[axis], pl.ds(first, rows)]
             own[...] = value[first : first + rows]
             for delta in (2, 1, 3):
-                self.push((stage, t, delta), own, self.device(axis, delta))
-
-    def push(self, key, view, device):
-        self.start(key, view, view, device)
+                self.copy(stage, stage, own, own, self.device(axis, delta)).start()
 
     def stage_end(self, stage):
-        parts = []
-        for t in range(3):
-            first, rows = GRAM_ROWS[t]
-            axis = ORDER[t][stage]
-            for delta in (1, 3, 2):
-                view = self.stages.at[stage, self.at(axis, 4 - delta), pl.ds(first, rows)]
-                self.wait((stage, t, delta), view)
-            slots = [self.stages[stage, p, first : first + rows] for p in range(RING)]
-            parts.append((slots[0] + slots[1]) + (slots[2] + slots[3]))
-        return jnp.concatenate(parts, axis=0)
+        self.wait(stage, self.stages.at[stage, pl.ds(0, 3)])
+        slots = [self.stages[stage, p] for p in range(RING)]
+        return (slots[0] + slots[1]) + (slots[2] + slots[3])
 
     def take(self, step):
-        (self.step_one, self.step_two, self.step_three, self.step_four, self.step_five)[step]()
-
-    def step_one(self):
-        self.wait("s", self.sibling_half)
-        self.stage_start(0, self.matrix[self.rows(self.core)] + self.sibling_half[...])
-
-    def step_two(self):
-        self.stage_start(1, self.stage_end(0))
-
-    def step_three(self):
-        self.stage_start(2, self.stage_end(1))
-
-    def step_four(self):
-        mine = self.total.at[self.rows(self.core)]
-        mine[...] = self.stage_end(2)
-        self.start("e", mine, mine, self.device())
-
-    def step_five(self):
-        self.wait("e", self.total.at[self.rows(1 - self.core)])
+        if step == 0:
+            self.wait("in", self.sibling_half)
+            self.stage_start(0, self.matrix[self.rows(self.core)] + self.sibling_half[...])
+        elif step < 3:
+            self.stage_start(step, self.stage_end(step - 1))
+        elif step == 3:
+            mine = self.total.at[self.rows(self.core)]
+            mine[...] = self.stage_end(2)
+            self.copy("out", "out", mine, mine, self.device()).start()
+        else:
+            self.wait("out", self.total.at[self.rows(1 - self.core)])
+
+    def finish(self):
+        for stage in range(3):
+            self.wait_sent(stage, self.stages.at[stage, pl.ds(0, 3)])
+        self.wait_sent("in", self.sibling_half)
+        self.wait_sent("out", self.total.at[self.rows(self.core)])
 
 
 def product(left, right, left_dim, right_dim):
@@ -483,7 +463,7 @@
             pltpu.VMEM((K, K), jnp.float32),
             *sums * 2,
             dma((8,)),
-            *[dma((COPIES,))] * 4,
+            *[dma((SENDS,)), dma((RECEIPTS,))] * 2,
             *[dma((SUMS,))] * 4,
         ],
         compiler_params=pltpu.CompilerParams(

time: 121 us -> 113 us (0.934)
  Pallas kernels: 120 us -> 111 us
    pallas_call x1, Pallas kernels: 114 us -> 105 us  [local(): pl.pallas_call(kernel, out_shape=(rows, square), in_specs=[anywhere] * 5,...]
where the time goes in v3:
time: 113 us; the launch traced here: 112 us
  Pallas kernels  111 us (98%)
  between operations  1.29 us (1%)
    pallas_call x1, Pallas kernels, local(): pl.pallas_call(kernel, out_shape=(rows, square), in_specs=[anywhere] * 5,...  105 us
    pallas_call x1, Pallas kernels, local(): pl.pallas_call(finish, out_shape=(rows, square), in_specs=[vmem] * 2, out...  6.21 us

profile of v3, /device:TPU:1, one launch (start us, length us, event | category | flops | bytes accessed | tf_op | source)
XLA Modules:
  0.0 112.4 jit_solution(1075589351168672906)
XLA Ops:
  1.3 104.9 %two_rounds.1 = (f32[512,128]{1,0:T(8,128)}, f32[128,128]{1,0:T(8,128)}) custom-call(s32[32]{0:T(128)} %cols_hbm.1, s32[1]{0:T(128)S(6)} %copy.7.live_hbm, bf16[32,512,512]{2,1,0:T(8,128)(2,1)} %tiles_hbm.1, s32[512]{0:T(512)} %degree_hbm.1, bf16[512,128]{1,0:T(8,128)(2,1)} %basis_hbm.1), custom_call_target="tpu_custom_call" | custom-call | tf_op jit(solution)/shard_map/two_rounds/pallas_call | solution.py:449
  106.2 6.2 %finish.1 = (f32[512,128]{1,0:T(8,128)}, f32[128,128]{1,0:T(8,128)}) custom-call(f32[512,128]{1,0:T(8,128)} %get-tuple-element.4.image, f32[128,128]{1,0:T(8,128)} %get-tuple-element.5.gram), custom_call_target="tpu_custom_call" | custom-call | tf_op jit(solution)/shard_map/finish/pallas_call | solution.py:474

commit v4 on v3

--- a/solution.py
+++ b/solution.py
@@ -21,27 +21,25 @@
 ROWS = (((0, 96), (96, 80), (176, 80)), ((0, 80), (80, 80), (160, 96)))
 GRAM_ROWS = ((0, 24), (24, 24), (48, 16))
 SENDS = 8
-RECEIPTS = 26
+RECEIPTS = 28
 SUMS = 5
 GROUP = 16
-WHOLE_ONE = ((False, False, False), (False, False, False))
-WHOLE_TWO = ((False, False, False), (False, False, False))
 ROUND_ONE = (
     ("first", 0), ("first", 1), ("line", 0), ("line", 1), ("plane", 0, 0), ("plane", 0, 1),
-    ("plane", 1, 0), ("plane", 1, 1), ("planed", 0), ("pass", 0, 0), ("pass", 0, 1), ("pass", 0, 2),
-    ("pass", 0, 3), ("planed", 1), ("pass", 1, 0), ("far", 0, 0), ("far", 0, 1), ("far", 0, 2),
-    ("pass", 1, 1), ("pass", 1, 2), ("far", 0, 3), ("pass", 1, 3), ("share", 0), ("loaded",),
+    ("plane", 1, 0), ("planed", 0), ("pass", 0, 0), ("plane", 1, 1), ("pass", 0, 1), ("pass", 0, 2),
+    ("far", 0, 0), ("pass", 0, 3), ("planed", 1), ("pass", 1, 0), ("far", 0, 1), ("far", 0, 2),
+    ("pass", 1, 1), ("far", 0, 3), ("pass", 1, 2), ("share", 0), ("pass", 1, 3), ("loaded",),
     ("multiply", 0, 0, 1), ("far", 1, 0), ("far", 1, 1), ("multiply", 0, 1, 2), ("far", 1, 2),
     ("far", 1, 3), ("share", 1),
 )
 ROUND_TWO = (
-    ("first", 0), ("half",), ("first", 1), ("line", 0), ("gram",), ("sum", 0), ("line", 1),
-    ("sum", 1), ("plane", 0, 0), ("plane", 0, 1), ("sum", 2), ("plane", 1, 0), ("plane", 1, 1),
-    ("planed", 0), ("sum", 3), ("pass", 0, 0), ("sum", 4), ("eliminate", 0), ("eliminate", 1),
-    ("eliminate", 2), ("pass", 0, 1), ("pass", 0, 2), ("pass", 0, 3), ("planed", 1), ("pass", 1, 0),
-    ("eliminate", 3), ("far", 0, 0), ("pass", 1, 1), ("far", 0, 1), ("far", 0, 2), ("far", 0, 3),
-    ("pass", 1, 2), ("share", 0), ("pass", 1, 3), ("multiply", 0, 0, 1), ("far", 1, 0),
-    ("far", 1, 1), ("multiply", 0, 1, 2), ("far", 1, 2), ("far", 1, 3), ("share", 1),
+    ("first", 0), ("half",), ("first", 1), ("line", 0), ("gram",), ("line", 1), ("sum", 0),
+    ("plane", 0, 0), ("plane", 0, 1), ("sum", 1), ("plane", 1, 0), ("plane", 1, 1), ("sum", 2),
+    ("planed", 0), ("planed", 1), ("pass", 0, 0), ("pass", 0, 1), ("sum", 3), ("pass", 0, 2),
+    ("sum", 4), ("eliminate", 0), ("pass", 0, 3), ("pass", 1, 0), ("eliminate", 1), ("pass", 1, 1),
+    ("pass", 1, 2), ("pass", 1, 3), ("far", 0, 0), ("eliminate", 2), ("far", 0, 1), ("far", 0, 2),
+    ("far", 0, 3), ("far", 1, 0), ("eliminate", 3), ("far", 1, 1), ("share", 0),
+    ("multiply", 0, 0, 1), ("far", 1, 2), ("far", 1, 3), ("multiply", 0, 1, 2), ("share", 1),
     ("multiply", 1, 0, 2),
 )
 
@@ -87,9 +85,9 @@
 
 
 class Gather(Links):
-    def __init__(self, waves, send, recv, whole):
+    def __init__(self, waves, send, recv):
         super().__init__(send, recv)
-        self.waves, self.whole = waves, whole
+        self.waves = waves
 
     def view(self, w, t, axes):
         first, rows = ROWS[w][t]
@@ -117,7 +115,19 @@
     def first_start(self, w):
         for t in range(3):
             for delta in (2, 1, 3):
-                self.push("first", "first", w, t, {}, self.device(ORDER[t][0], delta))
+                into = "opposite" if delta == 2 else "first"
+                self.push("first", into, w, t, {}, self.device(ORDER[t][0], delta))
+        self.block(w, {})
+
+    def block(self, w, *blocks):
+        for step in (1, 2):
+            for t in range(3):
+                for delta in (1, 3):
+                    into = ("second", delta) if step == 1 else ("third", 0)
+                    device = self.device(ORDER[t][step], delta)
+                    for axes in blocks:
+                        out = "second" if step == 1 else "third"
+                        self.push(out, into, w, t, axes if axes == {} else axes[t], device)
 
     def third_line(self, w, t, j):
         axes = self.line(t, self.seconds(t)[j])
@@ -126,22 +136,22 @@
         self.sibling(w, t, j, 0)
 
     def sibling(self, w, t, j, away):
-        third = self.at(ORDER[t][2], 4 - away)
-        if not self.whole[w][(0, 1, 2, 1)[away]]:
-            self.push("share", "share", w, t, self.line(t, self.seconds(t)[j], third), self.device())
-        elif j == 3:
-            self.push("share", "share", w, t, self.line(t, ALL, third), self.device())
+        axes = self.line(t, self.seconds(t)[j], self.at(ORDER[t][2], 4 - away))
+        self.push("share", "share", w, t, axes, self.device())
 
     def sibling_end(self, w):
         self.wait((w, "share"), self.blocks(w, 4, 4, 4))
 
     def first_end(self, w):
-        self.wait((w, "first"), self.blocks(w, 1, 1, 3))
-        for t in range(3):
-            for delta in (1, 3):
-                device = self.device(ORDER[t][1], delta)
-                self.push("second", ("second", delta), w, t, self.line(t), device)
-            self.third_line(w, t, 0)
+        from_start = [
+            [{ORDER[t][0]: self.at(ORDER[t][0], delta)} for t in range(3)] for delta in (3, 1, 2)
+        ]
+        self.wait((w, "first"), self.blocks(w, 1, 1, 2))
+        self.block(w, *from_start[:2])
+        self.wait((w, "opposite"), self.blocks(w, 1, 1, 1))
+        self.block(w, from_start[2])
+        for t in range(3):
+            self.sibling(w, t, 0, 0)
 
     def second_pass(self, w, k):
         delta, half = HALVES[k]
@@ -149,6 +159,7 @@
         for t in range(3):
             axes = self.line(t, self.seconds(t)[k + 1], half=half)
             self.push("second", "halves", w, t, axes, self.device(ORDER[t][1], delta))
+        for t in range(3):
             self.third_line(w, t, k + 1)
 
     def second_end(self, w):
@@ -163,6 +174,8 @@
             for delta, half in HALVES:
                 axes = self.line(t, source, self.at(axis, 4 - delta), half)
                 self.push("third", ("far", j), w, t, axes, self.device(axis, delta))
+        for t in range(3):
+            for delta in (1, 3):
                 self.sibling(w, t, j, delta)
 
     def third_end(self, w, j):
@@ -205,12 +218,15 @@
         self.copy("in", "in", out, self.sibling_half, self.device()).start()
 
     def stage_start(self, stage, value):
+        parts = []
         for t in range(3):
             first, rows = GRAM_ROWS[t]
             axis = ORDER[t][stage]
             own = self.stages.at[stage, self.pos[axis], pl.ds(first, rows)]
             own[...] = value[first : first + rows]
-            for delta in (2, 1, 3):
+            parts.append((axis, own))
+        for delta in (2, 1, 3):
+            for axis, own in parts:
                 self.copy(stage, stage, own, own, self.device(axis, delta)).start()
 
     def stage_end(self, stage):
@@ -323,8 +339,8 @@
     recv_h,
 ):
     items = float(BLK * 2 * RING**3)
-    first = Gather((a0, a1), send_a, recv_a, WHOLE_ONE)
-    second = Gather((b0, b1), send_b, recv_b, WHOLE_TWO)
+    first = Gather((a0, a1), send_a, recv_a)
+    second = Gather((b0, b1), send_b, recv_b)
     gram_one = Sum(half_one, stages_one, sum_one, send_g, recv_g)
     gram_two = Sum(half_two, stages_two, sum_two, send_h, recv_h)
     pos, core = first.pos, first.core
@@ -428,7 +444,7 @@
 
 def finish(image, gram, leading, factor):
     factors = []
-    for _ in factor_inverse(gram[...], factors):
+    for _ in factor_inverse(gram[...], factors, panel=64):
         pass
     upper, inverse = factors
     factor[...] = upper.T

time: 113 us -> 109 us (0.965)
  Pallas kernels: 111 us -> 107 us
    pallas_call x1, Pallas kernels: 105 us -> 102 us  [local(): pl.pallas_call(kernel, out_shape=(rows, square), in_specs=[anywhere] * 5,...]
where the time goes in v4:
time: 109 us
  Pallas kernels  107 us (98%)
  between operations  1.29 us (1%)
    pallas_call x1, Pallas kernels, local(): pl.pallas_call(kernel, out_shape=(rows, square), in_specs=[anywhere] * 5,...  102 us
    pallas_call x1, Pallas kernels, local(): pl.pallas_call(finish, out_shape=(rows, square), in_specs=[vmem] * 2, out...  5.76 us

profile of v4, /device:TPU:1, one launch (start us, length us, event | category | flops | bytes accessed | tf_op | source)
XLA Modules:
  0.0 108.7 jit_solution(6525433473757460674)
XLA Ops:
  1.3 101.6 %two_rounds.1 = (f32[512,128]{1,0:T(8,128)}, f32[128,128]{1,0:T(8,128)}) custom-call(s32[32]{0:T(128)} %cols_hbm.1, s32[1]{0:T(128)S(6)} %copy.7.live_hbm, bf16[32,512,512]{2,1,0:T(8,128)(2,1)} %tiles_hbm.1, s32[512]{0:T(512)} %degree_hbm.1, bf16[512,128]{1,0:T(8,128)(2,1)} %basis_hbm.1), custom_call_target="tpu_custom_call" | custom-call | tf_op jit(solution)/shard_map/two_rounds/pallas_call | solution.py:465
  102.9 5.8 %finish.1 = (f32[512,128]{1,0:T(8,128)}, f32[128,128]{1,0:T(8,128)}) custom-call(f32[512,128]{1,0:T(8,128)} %get-tuple-element.4.image, f32[128,128]{1,0:T(8,128)} %get-tuple-element.5.gram), custom_call_target="tpu_custom_call" | custom-call | tf_op jit(solution)/shard_map/finish/pallas_call | solution.py:490

commit v5 on v4

--- a/solution.py
+++ b/solution.py
@@ -11,36 +11,54 @@
 K = 128
 SLOTS = 32
 RING = 4
-WAVES = 2
+WAVES = 4
 DEPTH = BLK // WAVES
 MESH = pl.DeviceIdType.MESH
 HIGHEST = lax.Precision.HIGHEST
 ALL = pl.ds(0, RING)
 HALVES = ((1, pl.ds(0, 2)), (3, pl.ds(2, 2)))
 ORDER = ((1, 0, 2), (0, 2, 1), (2, 1, 0))
-ROWS = (((0, 96), (96, 80), (176, 80)), ((0, 80), (80, 80), (160, 96)))
+ROWS = (
+    ((0, 48), (48, 48), (96, 32)),
+    ((0, 32), (32, 48), (80, 48)),
+    ((0, 48), (48, 32), (80, 48)),
+    ((0, 48), (48, 48), (96, 32)),
+)
 GRAM_ROWS = ((0, 24), (24, 24), (48, 16))
-SENDS = 8
-RECEIPTS = 28
+SENDS = 4
+RECEIPTS = 56
 SUMS = 5
 GROUP = 16
+WHOLE = (0, 1, 2)
+EARLY = (0, 1)
 ROUND_ONE = (
-    ("first", 0), ("first", 1), ("line", 0), ("line", 1), ("plane", 0, 0), ("plane", 0, 1),
-    ("plane", 1, 0), ("planed", 0), ("pass", 0, 0), ("plane", 1, 1), ("pass", 0, 1), ("pass", 0, 2),
-    ("far", 0, 0), ("pass", 0, 3), ("planed", 1), ("pass", 1, 0), ("far", 0, 1), ("far", 0, 2),
-    ("pass", 1, 1), ("far", 0, 3), ("pass", 1, 2), ("share", 0), ("pass", 1, 3), ("loaded",),
-    ("multiply", 0, 0, 1), ("far", 1, 0), ("far", 1, 1), ("multiply", 0, 1, 2), ("far", 1, 2),
-    ("far", 1, 3), ("share", 1),
+    ("first", 0), ("first", 2), ("first", 1), ("first", 3), ("line", 0), ("line", 1), ("line", 2),
+    ("plane", 0, 0), ("plane", 0, 1), ("plane", 2, 0), ("plane", 1, 0), ("plane", 1, 1),
+    ("planed", 0), ("pass", 0, 0), ("plane", 2, 1), ("planed", 1), ("pass", 0, 1), ("line", 3),
+    ("pass", 0, 2), ("pass", 1, 0), ("pass", 0, 3), ("planed", 2), ("far", 0, 0), ("plane", 3, 0),
+    ("plane", 3, 1), ("pass", 2, 0), ("far", 0, 1), ("far", 1, 0), ("far", 0, 2), ("pass", 1, 1),
+    ("far", 0, 3), ("pass", 1, 2), ("pass", 1, 3), ("pass", 2, 1), ("share", 0), ("loaded",),
+    ("multiply", 0, 0, 1), ("planed", 3), ("pass", 2, 2), ("pass", 2, 3), ("multiply", 0, 1, 2),
+    ("far", 1, 1), ("far", 1, 2), ("pass", 3, 0), ("far", 1, 3), ("pass", 3, 1), ("far", 2, 0),
+    ("pass", 3, 2), ("far", 2, 1), ("pass", 3, 3), ("share", 1), ("multiply", 1, 0, 1),
+    ("far", 2, 2), ("far", 2, 3), ("multiply", 1, 1, 2), ("far", 3, 0), ("far", 3, 1), ("share", 2),
+    ("multiply", 2, 0, 1), ("far", 3, 2), ("far", 3, 3), ("multiply", 2, 1, 2), ("share", 3),
 )
 ROUND_TWO = (
-    ("first", 0), ("half",), ("first", 1), ("line", 0), ("gram",), ("line", 1), ("sum", 0),
-    ("plane", 0, 0), ("plane", 0, 1), ("sum", 1), ("plane", 1, 0), ("plane", 1, 1), ("sum", 2),
-    ("planed", 0), ("planed", 1), ("pass", 0, 0), ("pass", 0, 1), ("sum", 3), ("pass", 0, 2),
-    ("sum", 4), ("eliminate", 0), ("pass", 0, 3), ("pass", 1, 0), ("eliminate", 1), ("pass", 1, 1),
-    ("pass", 1, 2), ("pass", 1, 3), ("far", 0, 0), ("eliminate", 2), ("far", 0, 1), ("far", 0, 2),
-    ("far", 0, 3), ("far", 1, 0), ("eliminate", 3), ("far", 1, 1), ("share", 0),
-    ("multiply", 0, 0, 1), ("far", 1, 2), ("far", 1, 3), ("multiply", 0, 1, 2), ("share", 1),
-    ("multiply", 1, 0, 2),
+    ("first", 0), ("first", 1), ("half",), ("first", 2), ("first", 3), ("gram",), ("line", 0),
+    ("line", 1), ("sum", 0), ("line", 2), ("plane", 0, 0), ("plane", 0, 1), ("sum", 1),
+    ("plane", 1, 0), ("plane", 1, 1), ("planed", 0), ("pass", 0, 0), ("sum", 2), ("line", 3),
+    ("planed", 1), ("pass", 0, 1), ("pass", 0, 2), ("plane", 2, 0), ("plane", 2, 1), ("pass", 1, 0),
+    ("sum", 3), ("pass", 0, 3), ("plane", 3, 0), ("plane", 3, 1), ("sum", 4), ("far", 0, 0),
+    ("eliminate", 0), ("eliminate", 1), ("eliminate", 2), ("far", 0, 1), ("planed", 2),
+    ("far", 0, 2), ("pass", 1, 1), ("pass", 1, 2), ("far", 0, 3), ("pass", 1, 3), ("far", 1, 0),
+    ("pass", 2, 0), ("eliminate", 3), ("share", 0), ("planed", 3), ("pass", 2, 1), ("pass", 3, 0),
+    ("multiply", 0, 0, 1), ("pass", 2, 2), ("pass", 2, 3), ("far", 1, 1), ("far", 1, 2),
+    ("far", 1, 3), ("pass", 3, 1), ("pass", 3, 2), ("far", 2, 0), ("multiply", 0, 1, 2),
+    ("pass", 3, 3), ("far", 2, 1), ("share", 1), ("multiply", 1, 0, 1), ("far", 3, 0),
+    ("far", 2, 2), ("far", 2, 3), ("multiply", 1, 1, 2), ("far", 3, 1), ("far", 3, 2), ("share", 2),
+    ("multiply", 2, 0, 1), ("far", 3, 3), ("multiply", 2, 1, 2), ("share", 3),
+    ("multiply", 3, 0, 2),
 )
 
 
@@ -99,7 +117,7 @@
 
     def push(self, out, into, w, t, axes, device):
         view = self.view(w, t, axes)
-        self.copy((w, out), (w, into), view, view, device).start()
+        self.copy(out, (w, into), view, view, device).start()
 
     def line(self, t, second=None, third=None, half=ALL):
         axes = {ORDER[t][0]: half}
@@ -117,7 +135,8 @@
             for delta in (2, 1, 3):
                 into = "opposite" if delta == 2 else "first"
                 self.push("first", into, w, t, {}, self.device(ORDER[t][0], delta))
-        self.block(w, {})
+        if w in EARLY:
+            self.block(w, {})
 
     def block(self, w, *blocks):
         for step in (1, 2):
@@ -137,6 +156,10 @@
 
     def sibling(self, w, t, j, away):
         axes = self.line(t, self.seconds(t)[j], self.at(ORDER[t][2], 4 - away))
+        if w in WHOLE and away != 2:
+            if j < 3:
+                return
+            axes = self.line(t, ALL, self.at(ORDER[t][2], 4 - away))
         self.push("share", "share", w, t, axes, self.device())
 
     def sibling_end(self, w):
@@ -147,11 +170,20 @@
             [{ORDER[t][0]: self.at(ORDER[t][0], delta)} for t in range(3)] for delta in (3, 1, 2)
         ]
         self.wait((w, "first"), self.blocks(w, 1, 1, 2))
-        self.block(w, *from_start[:2])
+        if w in EARLY:
+            self.block(w, *from_start[:2])
         self.wait((w, "opposite"), self.blocks(w, 1, 1, 1))
-        self.block(w, from_start[2])
-        for t in range(3):
-            self.sibling(w, t, 0, 0)
+        if w in EARLY:
+            self.block(w, from_start[2])
+            for t in range(3):
+                self.sibling(w, t, 0, 0)
+            return
+        for t in range(3):
+            for delta in (1, 3):
+                device = self.device(ORDER[t][1], delta)
+                self.push("second", ("second", delta), w, t, self.line(t), device)
+        for t in range(3):
+            self.third_line(w, t, 0)
 
     def second_pass(self, w, k):
         delta, half = HALVES[k]
@@ -183,12 +215,11 @@
         for t in range(3):
             self.sibling(w, t, j, 2)
 
-    def finish(self):
-        for w in range(WAVES):
-            self.wait_sent((w, "first"), self.blocks(w, 1, 1, 3))
-            self.wait_sent((w, "second"), self.blocks(w, 1, 3, 4))
-            self.wait_sent((w, "third"), self.blocks(w, 3, 4, 4))
-            self.wait_sent((w, "share"), self.blocks(w, 4, 4, 4))
+    def finish(self, like):
+        self.wait_sent("first", like.at[0, pl.ds(0, 3 * K)])
+        self.wait_sent("second", like.at[pl.ds(0, 3)])
+        self.wait_sent("third", like.at[pl.ds(0, 12)])
+        self.wait_sent("share", like.at[pl.ds(0, 16)])
 
     def take(self, name, w, *more):
         step = {
@@ -317,8 +348,12 @@
     tiles,
     a0,
     a1,
+    a2,
+    a3,
     b0,
     b1,
+    b2,
+    b3,
     scale,
     total,
     gram,
@@ -339,8 +374,8 @@
     recv_h,
 ):
     items = float(BLK * 2 * RING**3)
-    first = Gather((a0, a1), send_a, recv_a)
-    second = Gather((b0, b1), send_b, recv_b)
+    first = Gather((a0, a1, a2, a3), send_a, recv_a)
+    second = Gather((b0, b1, b2, b3), send_b, recv_b)
     gram_one = Sum(half_one, stages_one, sum_one, send_g, recv_g)
     gram_two = Sum(half_two, stages_two, sum_two, send_h, recv_h)
     pos, core = first.pos, first.core
@@ -365,7 +400,7 @@
     loads[1].wait()
     for w in range(WAVES):
         rows = pl.ds(w * DEPTH, DEPTH)
-        place((a0, a1), w, scale[rows] * basis[rows].astype(jnp.float32))
+        place(first.waves, w, scale[rows] * basis[rows].astype(jnp.float32))
     pl.semaphore_wait(barrier, len(near))
 
     def multiply(waves, w, groups, rows=pl.ds(0, BLK)):
@@ -395,12 +430,14 @@
         else:
             first.take(name, *more)
 
-    def half_image(w):
-        rows = pl.ds(w * DEPTH, DEPTH)
-        multiply(first.waves, 1, (0, SLOTS // GROUP), rows)
+    def half_image(half):
+        rows = pl.ds(half * (BLK // 2), BLK // 2)
+        multiply(first.waves, WAVES - 1, (0, SLOTS // GROUP), rows)
         image = total[rows] * scale[rows]
         total[rows] = image
-        place((b0, b1), w, scale[rows] * image)
+        image = scale[rows] * image
+        for w in range(WAVES // 2):
+            place(second.waves, half * (WAVES // 2) + w, image[w * DEPTH : (w + 1) * DEPTH])
 
     factors = []
     half_image(0)
@@ -435,8 +472,8 @@
         gram_two.take(step)
     out_sum = pltpu.make_async_copy(sum_two, sum_hbm, load_sem.at[1])
     out_sum.start()
-    first.finish()
-    second.finish()
+    first.finish(tiles)
+    second.finish(tiles)
     gram_two.finish()
     out.wait()
     out_sum.wait()
@@ -473,7 +510,7 @@
             pltpu.VMEM((BLK,), jnp.int32),
             pltpu.VMEM((BLK, K), jnp.bfloat16),
             pltpu.VMEM((SLOTS, BLK, BLK), jnp.bfloat16),
-            *[wave] * 4,
+            *[wave] * (2 * WAVES),
             pltpu.VMEM((BLK, K), jnp.float32),
             pltpu.VMEM((BLK, K), jnp.float32),
             pltpu.VMEM((K, K), jnp.float32),

time: 109 us -> 107 us (0.982)
    pallas_call x1, Pallas kernels: 102 us -> 99.8 us  [local(): pl.pallas_call(kernel, out_shape=(rows, square), in_specs=[anywhere] * 5,...]
where the time goes in v5:
time: 107 us
  Pallas kernels  106 us (99%)
  between operations  1.29 us (1%)
    pallas_call x1, Pallas kernels, local(): pl.pallas_call(kernel, out_shape=(rows, square), in_specs=[anywhere] * 5,...  99.8 us
    pallas_call x1, Pallas kernels, local(): pl.pallas_call(finish, out_shape=(rows, square), in_specs=[vmem] * 2, out...  5.76 us

profile of v5, /device:TPU:1, one launch (start us, length us, event | category | flops | bytes accessed | tf_op | source)
XLA Modules:
  0.0 106.9 jit_solution(9187612985192525455)
XLA Ops:
  1.3 99.8 %two_rounds.1 = (f32[512,128]{1,0:T(8,128)}, f32[128,128]{1,0:T(8,128)}) custom-call(s32[32]{0:T(128)} %cols_hbm.1, s32[1]{0:T(128)S(6)} %copy.7.live_hbm, bf16[32,512,512]{2,1,0:T(8,128)(2,1)} %tiles_hbm.1, s32[512]{0:T(512)} %degree_hbm.1, bf16[512,128]{1,0:T(8,128)(2,1)} %basis_hbm.1), custom_call_target="tpu_custom_call" | custom-call | tf_op jit(solution)/shard_map/two_rounds/pallas_call | solution.py:502
  101.1 5.8 %finish.1 = (f32[512,128]{1,0:T(8,128)}, f32[128,128]{1,0:T(8,128)}) custom-call(f32[512,128]{1,0:T(8,128)} %get-tuple-element.4.image, f32[128,128]{1,0:T(8,128)} %get-tuple-element.5.gram), custom_call_target="tpu_custom_call" | custom-call | tf_op jit(solution)/shard_map/finish/pallas_call | solution.py:527

commit v6 on v5

--- a/solution.py
+++ b/solution.py
@@ -27,38 +27,38 @@
 GRAM_ROWS = ((0, 24), (24, 24), (48, 16))
 SENDS = 4
 RECEIPTS = 56
-SUMS = 5
+SUMS = 3
 GROUP = 16
 WHOLE = (0, 1, 2)
 EARLY = (0, 1)
 ROUND_ONE = (
     ("first", 0), ("first", 2), ("first", 1), ("first", 3), ("line", 0), ("line", 1), ("line", 2),
-    ("plane", 0, 0), ("plane", 0, 1), ("plane", 2, 0), ("plane", 1, 0), ("plane", 1, 1),
-    ("planed", 0), ("pass", 0, 0), ("plane", 2, 1), ("planed", 1), ("pass", 0, 1), ("line", 3),
-    ("pass", 0, 2), ("pass", 1, 0), ("pass", 0, 3), ("planed", 2), ("far", 0, 0), ("plane", 3, 0),
-    ("plane", 3, 1), ("pass", 2, 0), ("far", 0, 1), ("far", 1, 0), ("far", 0, 2), ("pass", 1, 1),
-    ("far", 0, 3), ("pass", 1, 2), ("pass", 1, 3), ("pass", 2, 1), ("share", 0), ("loaded",),
-    ("multiply", 0, 0, 1), ("planed", 3), ("pass", 2, 2), ("pass", 2, 3), ("multiply", 0, 1, 2),
-    ("far", 1, 1), ("far", 1, 2), ("pass", 3, 0), ("far", 1, 3), ("pass", 3, 1), ("far", 2, 0),
-    ("pass", 3, 2), ("far", 2, 1), ("pass", 3, 3), ("share", 1), ("multiply", 1, 0, 1),
-    ("far", 2, 2), ("far", 2, 3), ("multiply", 1, 1, 2), ("far", 3, 0), ("far", 3, 1), ("share", 2),
-    ("multiply", 2, 0, 1), ("far", 3, 2), ("far", 3, 3), ("multiply", 2, 1, 2), ("share", 3),
+    ("plane", 0, 0), ("plane", 0, 1), ("plane", 2, 0), ("line", 3), ("plane", 1, 0), ("planed", 0),
+    ("plane", 1, 1), ("pass", 0, 0), ("pass", 0, 1), ("plane", 2, 1), ("planed", 1), ("pass", 0, 2),
+    ("pass", 1, 0), ("pass", 0, 3), ("planed", 2), ("plane", 3, 0), ("plane", 3, 1), ("far", 0, 0),
+    ("far", 0, 1), ("pass", 1, 1), ("far", 0, 2), ("far", 1, 0), ("pass", 1, 2), ("far", 0, 3),
+    ("pass", 2, 0), ("pass", 1, 3), ("pass", 2, 1), ("share", 0), ("loaded",),
+    ("multiply", 0, 0, 1), ("planed", 3), ("pass", 2, 2), ("pass", 2, 3), ("pass", 3, 0),
+    ("far", 1, 1), ("multiply", 0, 1, 2), ("far", 1, 2), ("far", 1, 3), ("far", 2, 0),
+    ("pass", 3, 1), ("pass", 3, 2), ("share", 1), ("far", 2, 1), ("pass", 3, 3),
+    ("multiply", 1, 0, 1), ("far", 2, 2), ("far", 2, 3), ("multiply", 1, 1, 2), ("far", 3, 0),
+    ("far", 3, 1), ("share", 2), ("multiply", 2, 0, 1), ("far", 3, 2), ("far", 3, 3),
+    ("multiply", 2, 1, 2), ("share", 3),
 )
 ROUND_TWO = (
     ("first", 0), ("first", 1), ("half",), ("first", 2), ("first", 3), ("gram",), ("line", 0),
-    ("line", 1), ("sum", 0), ("line", 2), ("plane", 0, 0), ("plane", 0, 1), ("sum", 1),
-    ("plane", 1, 0), ("plane", 1, 1), ("planed", 0), ("pass", 0, 0), ("sum", 2), ("line", 3),
-    ("planed", 1), ("pass", 0, 1), ("pass", 0, 2), ("plane", 2, 0), ("plane", 2, 1), ("pass", 1, 0),
-    ("sum", 3), ("pass", 0, 3), ("plane", 3, 0), ("plane", 3, 1), ("sum", 4), ("far", 0, 0),
-    ("eliminate", 0), ("eliminate", 1), ("eliminate", 2), ("far", 0, 1), ("planed", 2),
-    ("far", 0, 2), ("pass", 1, 1), ("pass", 1, 2), ("far", 0, 3), ("pass", 1, 3), ("far", 1, 0),
-    ("pass", 2, 0), ("eliminate", 3), ("share", 0), ("planed", 3), ("pass", 2, 1), ("pass", 3, 0),
-    ("multiply", 0, 0, 1), ("pass", 2, 2), ("pass", 2, 3), ("far", 1, 1), ("far", 1, 2),
-    ("far", 1, 3), ("pass", 3, 1), ("pass", 3, 2), ("far", 2, 0), ("multiply", 0, 1, 2),
-    ("pass", 3, 3), ("far", 2, 1), ("share", 1), ("multiply", 1, 0, 1), ("far", 3, 0),
-    ("far", 2, 2), ("far", 2, 3), ("multiply", 1, 1, 2), ("far", 3, 1), ("far", 3, 2), ("share", 2),
-    ("multiply", 2, 0, 1), ("far", 3, 3), ("multiply", 2, 1, 2), ("share", 3),
-    ("multiply", 3, 0, 2),
+    ("line", 1), ("line", 2), ("sum", 0), ("plane", 0, 0), ("line", 3), ("plane", 0, 1), ("sum", 1),
+    ("plane", 1, 0), ("plane", 1, 1), ("planed", 0), ("plane", 2, 0), ("pass", 0, 0), ("planed", 1),
+    ("pass", 0, 1), ("plane", 2, 1), ("pass", 0, 2), ("pass", 1, 0), ("sum", 2), ("plane", 3, 0),
+    ("pass", 1, 1), ("eliminate", 0), ("eliminate", 1), ("pass", 0, 3), ("eliminate", 2),
+    ("plane", 3, 1), ("pass", 1, 2), ("planed", 2), ("eliminate", 3), ("far", 1, 0), ("pass", 1, 3),
+    ("far", 0, 0), ("far", 0, 1), ("far", 0, 2), ("pass", 2, 0), ("far", 0, 3), ("far", 1, 1),
+    ("planed", 3), ("pass", 2, 1), ("pass", 3, 0), ("share", 0), ("multiply", 0, 0, 1),
+    ("far", 1, 2), ("pass", 2, 2), ("pass", 2, 3), ("far", 1, 3), ("pass", 3, 1), ("pass", 3, 2),
+    ("multiply", 0, 1, 2), ("pass", 3, 3), ("far", 2, 0), ("far", 2, 1), ("share", 1),
+    ("multiply", 1, 0, 1), ("far", 2, 2), ("far", 3, 0), ("far", 2, 3), ("multiply", 1, 1, 2),
+    ("far", 3, 1), ("share", 2), ("far", 3, 2), ("multiply", 2, 0, 1), ("far", 3, 3),
+    ("multiply", 2, 1, 2), ("share", 3), ("multiply", 3, 0, 2),
 )
 
 
@@ -76,12 +76,12 @@
     def at(self, axis, delta):
         return lax.rem(self.pos[axis] + delta, RING)
 
-    def device(self, axis=None, delta=0):
+    def device(self, axis=None, delta=0, core=None):
         place = list(self.pos)
-        core = self.core
         if axis is None:
-            core = 1 - core
+            core = 1 - self.core
         else:
+            core = self.core if core is None else core
             place[axis] = self.at(axis, delta)
         return (place[0] * RING + place[1], place[2] * 2 + core)
 
@@ -235,54 +235,65 @@
 
 
 class Sum(Links):
-    def __init__(self, sibling_half, stages, total, send, recv):
+    def __init__(self, stages, send, recv):
         super().__init__(send, recv)
-        self.sibling_half, self.stages, self.total = sibling_half, stages, total
+        self.stages = stages
         self.half = K // 2
 
-    def rows(self, core):
-        return pl.ds(pl.multiple_of(core * self.half, self.half), self.half)
+    def spread(self, stage, parts):
+        for delta in (2, 1, 3):
+            for axis, copies in parts:
+                for core, source, target in copies:
+                    self.copy(stage, stage, source, target, self.device(axis, delta, core)).start()
 
     def begin(self, matrix):
-        self.matrix = matrix
-        out = matrix.at[self.rows(1 - self.core)]
-        self.copy("in", "in", out, self.sibling_half, self.device()).start()
+        parts = []
+        for t in range(3):
+            first, rows = GRAM_ROWS[t]
+            axis = ORDER[t][0]
+            target = self.stages[0].at[self.pos[axis] * 2 + self.core, pl.ds(first, rows)]
+            copies = []
+            for core in (self.core, 1 - self.core):
+                start = pl.multiple_of(core * self.half + first, 8)
+                copies.append((core, matrix.at[pl.ds(start, rows)], target))
+            target[...] = copies[0][1][...]
+            self.copy(0, 0, copies[1][1], target, self.device()).start()
+            parts.append((axis, copies))
+        self.spread(0, parts)
 
     def stage_start(self, stage, value):
         parts = []
         for t in range(3):
             first, rows = GRAM_ROWS[t]
             axis = ORDER[t][stage]
-            own = self.stages.at[stage, self.pos[axis], pl.ds(first, rows)]
+            slot = self.pos[axis] if stage == 1 else self.core * RING + self.pos[axis]
+            own = self.stages[stage].at[slot, pl.ds(first, rows)]
             own[...] = value[first : first + rows]
-            parts.append((axis, own))
-        for delta in (2, 1, 3):
-            for axis, own in parts:
-                self.copy(stage, stage, own, own, self.device(axis, delta)).start()
+            if stage == 2:
+                self.copy(2, 2, own, own, self.device()).start()
+            cores = (self.core,) if stage == 1 else (self.core, 1 - self.core)
+            parts.append((axis, [(core, own, own) for core in cores]))
+        self.spread(stage, parts)
 
     def stage_end(self, stage):
-        self.wait(stage, self.stages.at[stage, pl.ds(0, 3)])
-        slots = [self.stages[stage, p] for p in range(RING)]
-        return (slots[0] + slots[1]) + (slots[2] + slots[3])
+        slots = self.stages[stage]
+        count = slots.shape[0]
+        self.wait(stage, slots.at[pl.ds(0, count - 1)])
+        sums = [slots[2 * i] + slots[2 * i + 1] for i in range(count // 2)]
+        return [sums[2 * i] + sums[2 * i + 1] for i in range(count // 4)]
 
     def take(self, step):
+        parts = self.stage_end(step)
         if step == 0:
-            self.wait("in", self.sibling_half)
-            self.stage_start(0, self.matrix[self.rows(self.core)] + self.sibling_half[...])
-        elif step < 3:
-            self.stage_start(step, self.stage_end(step - 1))
-        elif step == 3:
-            mine = self.total.at[self.rows(self.core)]
-            mine[...] = self.stage_end(2)
-            self.copy("out", "out", mine, mine, self.device()).start()
+            self.stage_start(1, parts[0] + parts[1])
+        elif step == 1:
+            self.stage_start(2, parts[0])
         else:
-            self.wait("out", self.total.at[self.rows(1 - self.core)])
+            self.total = jnp.concatenate(parts, axis=0)
 
     def finish(self):
-        for stage in range(3):
-            self.wait_sent(stage, self.stages.at[stage, pl.ds(0, 3)])
-        self.wait_sent("in", self.sibling_half)
-        self.wait_sent("out", self.total.at[self.rows(self.core)])
+        for stage, slots in enumerate(self.stages):
+            self.wait_sent(stage, slots.at[pl.ds(0, slots.shape[0] - 1)])
 
 
 def product(left, right, left_dim, right_dim):
@@ -298,14 +309,16 @@
     uppers, inverses = [], []
     for first in range(0, K, panel):
         a, w = matrix[:panel], side[:panel]
+        done_a, done_w = [], []
         for j in range(0, panel, pivots):
-            span = range(pivots)
-            cols = [
-                jnp.broadcast_to(a[:, first + j + q : first + j + q + 1], (panel, K)) for q in span
-            ]
-            row_a = [a[j + q : j + q + 1] for q in span]
-            row_w = [w[j + q : j + q + 1] for q in span]
-            small = [[cols[k][j + q : j + q + 1] for k in span] for q in span]
+            span, left = range(pivots), panel - j
+            at = first + j
+            cols = [jnp.broadcast_to(a[:, at + q : at + q + 1], (left, K)) for q in span]
+            row_a, row_w = [a[q : q + 1] for q in span], [w[q : q + 1] for q in span]
+            small = [[cols[k][q : q + 1] for k in span] for q in span]
+            below = left > pivots
+            if below:
+                cols, a, w = [col[pivots:] for col in cols], a[pivots:], w[pivots:]
             for q in span:
                 inverse = 1.0 / small[q][q]
                 ratio = {k: small[q][k] * inverse for k in range(q + 1, pivots)}
@@ -314,15 +327,17 @@
                         small[k][m] = small[k][m] - ratio[k] * small[q][m]
                     row_a[k] = row_a[k] - ratio[k] * row_a[q]
                     row_w[k] = row_w[k] - ratio[k] * row_w[q]
-                weight = jnp.where(row > j + q, cols[q], 0.0) * inverse
-                for k in range(q + 1, pivots):
-                    cols[k] = cols[k] - cols[q] * ratio[k]
-                a = a - weight * row_a[q]
-                w = w - weight * row_w[q]
-        diagonal = jnp.sum(jnp.where(lane == row + first, a, 0.0), axis=1, keepdims=True)
-        scale = lax.rsqrt(diagonal)
-        a = jnp.where(lane >= row + first, a * scale, 0.0)
-        w = w * scale
+                if below:
+                    weight = cols[q] * inverse
+                    for k in range(q + 1, pivots):
+                        cols[k] = cols[k] - cols[q] * ratio[k]
+                    a = a - weight * row_a[q]
+                    w = w - weight * row_w[q]
+                root = lax.rsqrt(small[q][q])
+                done_a.append(row_a[q] * root)
+                done_w.append(row_w[q] * root)
+        a = jnp.where(lane >= row + first, jnp.concatenate(done_a, axis=0), 0.0)
+        w = jnp.concatenate(done_w, axis=0)
         uppers.append(a)
         inverses.append(w)
         if first + panel < K:
@@ -357,12 +372,13 @@
     scale,
     total,
     gram,
-    half_one,
-    stages_one,
-    sum_one,
-    half_two,
-    stages_two,
-    sum_two,
+    summed,
+    one_first,
+    one_second,
+    one_third,
+    two_first,
+    two_second,
+    two_third,
     load_sem,
     send_a,
     recv_a,
@@ -376,12 +392,17 @@
     items = float(BLK * 2 * RING**3)
     first = Gather((a0, a1, a2, a3), send_a, recv_a)
     second = Gather((b0, b1, b2, b3), send_b, recv_b)
-    gram_one = Sum(half_one, stages_one, sum_one, send_g, recv_g)
-    gram_two = Sum(half_two, stages_two, sum_two, send_h, recv_h)
+    gram_one = Sum((one_first, one_second, one_third), send_g, recv_g)
+    gram_two = Sum((two_first, two_second, two_third), send_h, recv_h)
     pos, core = first.pos, first.core
 
     barrier = pltpu.get_barrier_semaphore()
-    near = [first.device()] + [first.device(axis, d) for axis in range(3) for d in (1, 2, 3)]
+    near = [first.device()] + [
+        first.device(axis, delta, c)
+        for c in (core, 1 - core)
+        for axis in range(3)
+        for delta in (1, 2, 3)
+    ]
     for device in near:
         pl.semaphore_signal(barrier, inc=1, device_id=device, device_id_type=MESH)
     pairs = [(degree_hbm, degree), (basis_hbm, basis), (cols_hbm, cols), (live_hbm, live)]
@@ -453,7 +474,7 @@
             gram_one.take(more[0])
         elif name == "eliminate":
             if more[0] == 0:
-                elimination = factor_inverse(sum_one[...], factors)
+                elimination = factor_inverse(gram_one.total, factors)
             next(elimination)
         elif name == "multiply":
             multiply(second.waves, more[0], more[1:])
@@ -468,9 +489,10 @@
     gram_one.finish()
     gram[...] = product(image, image, 0, 0) * (1.0 / items)
     gram_two.begin(gram)
-    for step in range(5):
+    for step in range(3):
         gram_two.take(step)
-    out_sum = pltpu.make_async_copy(sum_two, sum_hbm, load_sem.at[1])
+    summed[...] = gram_two.total
+    out_sum = pltpu.make_async_copy(summed, sum_hbm, load_sem.at[1])
     out_sum.start()
     first.finish(tiles)
     second.finish(tiles)
@@ -492,9 +514,9 @@
     vmem, anywhere = pl.BlockSpec(memory_space=pltpu.VMEM), pl.BlockSpec(memory_space=pl.ANY)
     wave = pltpu.VMEM((RING, RING, RING, 2, DEPTH, K), jnp.bfloat16)
     sums = [
-        pltpu.VMEM((K // 2, K), jnp.float32),
-        pltpu.VMEM((3, RING, K // 2, K), jnp.float32),
-        pltpu.VMEM((K, K), jnp.float32),
+        pltpu.VMEM((2 * RING, K // 2, K), jnp.float32),
+        pltpu.VMEM((RING, K // 2, K), jnp.float32),
+        pltpu.VMEM((2 * RING, K // 2, K), jnp.float32),
     ]
     dma = pltpu.SemaphoreType.DMA
     rows = jax.ShapeDtypeStruct((BLK, K), jnp.float32)
@@ -514,6 +536,7 @@
             pltpu.VMEM((BLK, K), jnp.float32),
             pltpu.VMEM((BLK, K), jnp.float32),
             pltpu.VMEM((K, K), jnp.float32),
+            pltpu.VMEM((K, K), jnp.float32),
             *sums * 2,
             dma((8,)),
             *[dma((SENDS,)), dma((RECEIPTS,))] * 2,

time: 107 us -> 106 us (level)
  no operation moved by 1% of the time
where the time goes in v6:
time: 106 us
  Pallas kernels  105 us (99%)
  between operations  1.29 us (1%)
    pallas_call x1, Pallas kernels, local(): pl.pallas_call(kernel, out_shape=(rows, square), in_specs=[anywhere] * 5,...  99.3 us
    pallas_call x1, Pallas kernels, local(): pl.pallas_call(finish, out_shape=(rows, square), in_specs=[vmem] * 2, out...  5.45 us

profile of v6, /device:TPU:1, one launch (start us, length us, event | category | flops | bytes accessed | tf_op | source)
XLA Modules:
  0.0 106.1 jit_solution(15941885300858305735)
XLA Ops:
  1.3 99.3 %two_rounds.1 = (f32[512,128]{1,0:T(8,128)}, f32[128,128]{1,0:T(8,128)}) custom-call(s32[32]{0:T(128)} %cols_hbm.1, s32[1]{0:T(128)S(6)} %copy.7.live_hbm, bf16[32,512,512]{2,1,0:T(8,128)(2,1)} %tiles_hbm.1, s32[512]{0:T(512)} %degree_hbm.1, bf16[512,128]{1,0:T(8,128)(2,1)} %basis_hbm.1), custom_call_target="tpu_custom_call" | custom-call | tf_op jit(solution)/shard_map/two_rounds/pallas_call | solution.py:524
  100.6 5.4 %finish.1 = (f32[512,128]{1,0:T(8,128)}, f32[128,128]{1,0:T(8,128)}) custom-call(f32[512,128]{1,0:T(8,128)} %get-tuple-element.4.image, f32[128,128]{1,0:T(8,128)} %get-tuple-element.5.gram), custom_call_target="tpu_custom_call" | custom-call | tf_op jit(solution)/shard_map/finish/pallas_call | solution.py:550

commit v7 on v6

--- a/solution.py
+++ b/solution.py
@@ -29,35 +29,35 @@
 RECEIPTS = 56
 SUMS = 3
 GROUP = 16
-WHOLE = (0, 1, 2)
-EARLY = (0, 1)
+WHOLE = (0, 1)
+EARLY = (0, 1, 2)
 ROUND_ONE = (
-    ("first", 0), ("first", 2), ("first", 1), ("first", 3), ("line", 0), ("line", 1), ("line", 2),
-    ("plane", 0, 0), ("plane", 0, 1), ("plane", 2, 0), ("line", 3), ("plane", 1, 0), ("planed", 0),
-    ("plane", 1, 1), ("pass", 0, 0), ("pass", 0, 1), ("plane", 2, 1), ("planed", 1), ("pass", 0, 2),
-    ("pass", 1, 0), ("pass", 0, 3), ("planed", 2), ("plane", 3, 0), ("plane", 3, 1), ("far", 0, 0),
-    ("far", 0, 1), ("pass", 1, 1), ("far", 0, 2), ("far", 1, 0), ("pass", 1, 2), ("far", 0, 3),
-    ("pass", 2, 0), ("pass", 1, 3), ("pass", 2, 1), ("share", 0), ("loaded",),
-    ("multiply", 0, 0, 1), ("planed", 3), ("pass", 2, 2), ("pass", 2, 3), ("pass", 3, 0),
-    ("far", 1, 1), ("multiply", 0, 1, 2), ("far", 1, 2), ("far", 1, 3), ("far", 2, 0),
-    ("pass", 3, 1), ("pass", 3, 2), ("share", 1), ("far", 2, 1), ("pass", 3, 3),
+    ("first", 2), ("first", 0), ("first", 1), ("first", 3), ("line", 2), ("line", 0), ("line", 1),
+    ("line", 3), ("plane", 0, 0), ("plane", 2, 0), ("plane", 0, 1), ("plane", 1, 0),
+    ("plane", 2, 1), ("plane", 1, 1), ("planed", 0), ("pass", 0, 0), ("plane", 3, 0),
+    ("pass", 0, 1), ("planed", 1), ("plane", 3, 1), ("planed", 2), ("pass", 0, 2), ("far", 0, 0),
+    ("pass", 0, 3), ("pass", 1, 0), ("pass", 1, 1), ("pass", 1, 2), ("pass", 2, 0), ("far", 0, 1),
+    ("pass", 1, 3), ("planed", 3), ("pass", 2, 1), ("pass", 2, 2), ("pass", 2, 3), ("pass", 3, 0),
+    ("far", 0, 2), ("far", 0, 3), ("pass", 3, 1), ("far", 1, 0), ("far", 1, 1), ("pass", 3, 2),
+    ("far", 1, 2), ("share", 0), ("loaded",), ("multiply", 0, 0, 1), ("far", 1, 3),
+    ("multiply", 0, 1, 2), ("pass", 3, 3), ("far", 2, 0), ("share", 1), ("far", 2, 1),
     ("multiply", 1, 0, 1), ("far", 2, 2), ("far", 2, 3), ("multiply", 1, 1, 2), ("far", 3, 0),
-    ("far", 3, 1), ("share", 2), ("multiply", 2, 0, 1), ("far", 3, 2), ("far", 3, 3),
+    ("share", 2), ("far", 3, 1), ("multiply", 2, 0, 1), ("far", 3, 2), ("far", 3, 3),
     ("multiply", 2, 1, 2), ("share", 3),
 )
 ROUND_TWO = (
-    ("first", 0), ("first", 1), ("half",), ("first", 2), ("first", 3), ("gram",), ("line", 0),
-    ("line", 1), ("line", 2), ("sum", 0), ("plane", 0, 0), ("line", 3), ("plane", 0, 1), ("sum", 1),
-    ("plane", 1, 0), ("plane", 1, 1), ("planed", 0), ("plane", 2, 0), ("pass", 0, 0), ("planed", 1),
-    ("pass", 0, 1), ("plane", 2, 1), ("pass", 0, 2), ("pass", 1, 0), ("sum", 2), ("plane", 3, 0),
-    ("pass", 1, 1), ("eliminate", 0), ("eliminate", 1), ("pass", 0, 3), ("eliminate", 2),
-    ("plane", 3, 1), ("pass", 1, 2), ("planed", 2), ("eliminate", 3), ("far", 1, 0), ("pass", 1, 3),
-    ("far", 0, 0), ("far", 0, 1), ("far", 0, 2), ("pass", 2, 0), ("far", 0, 3), ("far", 1, 1),
-    ("planed", 3), ("pass", 2, 1), ("pass", 3, 0), ("share", 0), ("multiply", 0, 0, 1),
-    ("far", 1, 2), ("pass", 2, 2), ("pass", 2, 3), ("far", 1, 3), ("pass", 3, 1), ("pass", 3, 2),
-    ("multiply", 0, 1, 2), ("pass", 3, 3), ("far", 2, 0), ("far", 2, 1), ("share", 1),
-    ("multiply", 1, 0, 1), ("far", 2, 2), ("far", 3, 0), ("far", 2, 3), ("multiply", 1, 1, 2),
-    ("far", 3, 1), ("share", 2), ("far", 3, 2), ("multiply", 2, 0, 1), ("far", 3, 3),
+    ("first", 0), ("first", 1), ("half",), ("first", 3), ("first", 2), ("gram",), ("line", 0),
+    ("line", 1), ("line", 3), ("plane", 0, 0), ("plane", 0, 1), ("sum", 0), ("plane", 1, 0),
+    ("plane", 1, 1), ("line", 2), ("sum", 1), ("planed", 0), ("pass", 0, 0), ("planed", 1),
+    ("pass", 0, 1), ("plane", 2, 0), ("pass", 0, 2), ("pass", 1, 0), ("sum", 2), ("eliminate", 0),
+    ("plane", 2, 1), ("eliminate", 1), ("pass", 1, 1), ("pass", 0, 3), ("far", 0, 0), ("far", 0, 1),
+    ("plane", 3, 0), ("plane", 3, 1), ("eliminate", 2), ("planed", 2), ("eliminate", 3),
+    ("far", 0, 2), ("pass", 2, 0), ("far", 0, 3), ("far", 1, 0), ("pass", 1, 2), ("pass", 1, 3),
+    ("share", 0), ("far", 1, 1), ("planed", 3), ("pass", 2, 1), ("multiply", 0, 0, 1),
+    ("pass", 2, 2), ("pass", 2, 3), ("pass", 3, 0), ("pass", 3, 1), ("far", 2, 0), ("far", 1, 2),
+    ("far", 1, 3), ("pass", 3, 2), ("multiply", 0, 1, 2), ("pass", 3, 3), ("far", 2, 1),
+    ("share", 1), ("multiply", 1, 0, 1), ("far", 2, 2), ("far", 2, 3), ("multiply", 1, 1, 2),
+    ("far", 3, 0), ("far", 3, 1), ("share", 2), ("multiply", 2, 0, 1), ("far", 3, 2), ("far", 3, 3),
     ("multiply", 2, 1, 2), ("share", 3), ("multiply", 3, 0, 2),
 )
 

time: 106 us -> 105 us (level)
  no operation moved by 1% of the time
where the time goes in v7:
time: 105 us
  Pallas kernels  104 us (99%)
  between operations  1.29 us (1%)
    pallas_call x1, Pallas kernels, local(): pl.pallas_call(kernel, out_shape=(rows, square), in_specs=[anywhere] * 5,...  98.5 us
    pallas_call x1, Pallas kernels, local(): pl.pallas_call(finish, out_shape=(rows, square), in_specs=[vmem] * 2, out...  5.45 us

profile of v7, /device:TPU:1, one launch (start us, length us, event | category | flops | bytes accessed | tf_op | source)
XLA Modules:
  0.0 105.2 jit_solution(14632500963750827662)
XLA Ops:
  1.3 98.5 %two_rounds.1 = (f32[512,128]{1,0:T(8,128)}, f32[128,128]{1,0:T(8,128)}) custom-call(s32[32]{0:T(128)} %cols_hbm.1, s32[1]{0:T(128)S(6)} %copy.7.live_hbm, bf16[32,512,512]{2,1,0:T(8,128)(2,1)} %tiles_hbm.1, s32[512]{0:T(512)} %degree_hbm.1, bf16[512,128]{1,0:T(8,128)(2,1)} %basis_hbm.1), custom_call_target="tpu_custom_call" | custom-call | tf_op jit(solution)/shard_map/two_rounds/pallas_call | solution.py:524
  99.8 5.4 %finish.1 = (f32[512,128]{1,0:T(8,128)}, f32[128,128]{1,0:T(8,128)}) custom-call(f32[512,128]{1,0:T(8,128)} %get-tuple-element.4.image, f32[128,128]{1,0:T(8,128)} %get-tuple-element.5.gram), custom_call_target="tpu_custom_call" | custom-call | tf_op jit(solution)/shard_map/finish/pallas_call | solution.py:550

commit v8 on v7

--- a/solution.py
+++ b/solution.py
@@ -424,12 +424,12 @@
         place(first.waves, w, scale[rows] * basis[rows].astype(jnp.float32))
     pl.semaphore_wait(barrier, len(near))
 
-    def multiply(waves, w, groups, rows=pl.ds(0, BLK)):
+    def multiply(waves, w, groups, rows=pl.ds(0, BLK), size=GROUP):
         @pl.loop(*groups)
         def _(group):
             parts = []
-            for u in range(GROUP):
-                slot = group * GROUP + u
+            for u in range(size):
+                slot = group * size + u
                 col = cols[slot]
                 picked = waves[w][
                     col // 32, lax.rem(col // 8, 4), lax.rem(col // 2, 4), lax.rem(col, 2)
@@ -453,7 +453,7 @@
 
     def half_image(half):
         rows = pl.ds(half * (BLK // 2), BLK // 2)
-        multiply(first.waves, WAVES - 1, (0, SLOTS // GROUP), rows)
+        multiply(first.waves, WAVES - 1, (0, 1), rows, SLOTS)
         image = total[rows] * scale[rows]
         total[rows] = image
         image = scale[rows] * image

time: 105 us -> 106 us (level)
  no operation moved by 1% of the time
where the time goes in v8:
time: 106 us; the launch traced here: 105 us
  Pallas kernels  104 us (98%)
  between operations  1.29 us (1%)
    pallas_call x1, Pallas kernels, local(): pl.pallas_call(kernel, out_shape=(rows, square), in_specs=[anywhere] * 5,...  98.7 us
    pallas_call x1, Pallas kernels, local(): pl.pallas_call(finish, out_shape=(rows, square), in_specs=[vmem] * 2, out...  5.45 us

profile of v8, /device:TPU:1, one launch (start us, length us, event | category | flops | bytes accessed | tf_op | source)
XLA Modules:
  0.0 105.4 jit_solution(16115051375810208570)
XLA Ops:
  1.3 98.7 %two_rounds.1 = (f32[512,128]{1,0:T(8,128)}, f32[128,128]{1,0:T(8,128)}) custom-call(s32[32]{0:T(128)} %cols_hbm.1, s32[1]{0:T(128)S(6)} %copy.7.live_hbm, bf16[32,512,512]{2,1,0:T(8,128)(2,1)} %tiles_hbm.1, s32[512]{0:T(512)} %degree_hbm.1, bf16[512,128]{1,0:T(8,128)(2,1)} %basis_hbm.1), custom_call_target="tpu_custom_call" | custom-call | tf_op jit(solution)/shard_map/two_rounds/pallas_call | solution.py:524
  100.0 5.4 %finish.1 = (f32[512,128]{1,0:T(8,128)}, f32[128,128]{1,0:T(8,128)}) custom-call(f32[512,128]{1,0:T(8,128)} %get-tuple-element.4.image, f32[128,128]{1,0:T(8,128)} %get-tuple-element.5.gram), custom_call_target="tpu_custom_call" | custom-call | tf_op jit(solution)/shard_map/finish/pallas_call | solution.py:550
